TPU v7x, 256 devices: a whole 4x4x8 slice. The times are simulated.
256 devices in a mesh: patch: 64 (over y, z, x_hi), tensor: 4 (over x_lo, core).
Axes of the slice: x: 4 (x_hi: 2, x_lo: 2; x = x_hi * 2 + x_lo), y: 4, z: 8, core: 2. Of those that a mesh axis runs over, the one named last changes fastest.
Arguments:
- hidden: bfloat16 [8192, 5120], P('patch'), may hold values from -24 to 24
- query: bfloat16 [8192, 2560], P('patch', 'tensor'), may hold values from -16 to 16
- query_gain: float32 [2560], P('tensor'), may hold values from 0.7 to 3.5
- stale_keys: bfloat16 [8192, 2560], P('patch', 'tensor'), may hold values from -192 to 192
- stale_values: bfloat16 [8192, 2560], P('patch', 'tensor'), may hold values from -6 to 6
- out_weight: bfloat16 [2560, 5120], P('tensor'), may hold values from -0.125 to 0.125
- out_bias: float32 [5120], replicated, may hold values from -3 to 3
- residual_gate: float32 [5120], replicated, may hold values from 0.5 to 4
- norm_shift: float32 [5120], replicated, may hold values from -4 to 4
- norm_scale: float32 [5120], replicated, may hold values from -2 to 2
Outputs:
- residual: bfloat16 [8192, 5120], P('patch', 'tensor')
- modulated: bfloat16 [8192, 5120], P('patch', 'tensor')
All inputs are finite; a program needn't handle non-finite values.
Results may differ from a plain program's by a relative error of at most 0.0071.
Values may be sent and summed in bfloat16 or wider, within the bound.
A program may use at most 128 MiB of HBM per device.

v0:
```python
import jax
import jax.numpy as jnp
from jax import lax
from jax.sharding import PartitionSpec as P

D = 5120
HEAD = 128
HD = 2560


def body(
    hidden,
    query,
    query_gain,
    stale_keys,
    stale_values,
    out_weight,
    out_bias,
    residual_gate,
    norm_shift,
    norm_scale,
):
    rows_here, width_here = query.shape
    heads_here = width_here // HEAD
    query_wide = query.astype(jnp.float32)
    squares = lax.psum(jnp.sum(query_wide * query_wide, axis=1), "tensor")
    query_rms = jnp.sqrt(squares / HD + 1e-06)
    normed_query = (query_wide / query_rms[:, None] * query_gain).astype(jnp.bfloat16)
    normed_query = normed_query.reshape(rows_here, heads_here, HEAD)
    factor = HEAD ** (-0.5)
    all_keys, all_values = (
        lax.all_gather(stale_keys, "patch", axis=0, tiled=True),
        lax.all_gather(stale_values, "patch", axis=0, tiled=True),
    )
    pieces = (all_keys, all_values)
    top = jnp.full((heads_here, rows_here), -1e30, jnp.float32)
    keys_piece = pieces[0].reshape(pieces[0].shape[0], heads_here, HEAD)
    values_piece = pieces[1].reshape(pieces[1].shape[0], heads_here, HEAD)
    scores = (
        jnp.einsum("thc,jhc->htj", normed_query, keys_piece, preferred_element_type=jnp.float32)
        * factor
    )
    new_top = jnp.maximum(top, jnp.max(scores, axis=2))
    expo = jnp.exp(scores - new_top[:, :, None])
    totals = jnp.sum(expo, axis=2)
    accum = jnp.einsum(
        "htj,jhc->htc", expo.astype(jnp.bfloat16), values_piece, preferred_element_type=jnp.float32
    )
    top, totals, accum = (new_top, totals, accum)
    attended = (
        jnp.transpose(accum / totals[:, :, None], (1, 0, 2))
        .reshape(rows_here, width_here)
        .astype(jnp.bfloat16)
    )
    partial_out = jnp.dot(attended, out_weight, preferred_element_type=jnp.float32)
    columns = D // lax.axis_size("tensor")
    first_col = lax.axis_index("tensor") * columns
    full_branch = lax.psum(partial_out, "tensor")
    summed = hidden.astype(jnp.float32) + residual_gate * (full_branch + out_bias)
    row_mean = jnp.sum(summed, axis=1) / D
    row_var = jnp.sum(summed * summed, axis=1) / D - row_mean * row_mean
    modulated = (summed - row_mean[:, None]) / jnp.sqrt(row_var[:, None] + 1e-06) * (
        1.0 + norm_scale
    ) + norm_shift
    summed_part = lax.dynamic_slice_in_dim(summed, first_col, columns, 1)
    modulated_part = lax.dynamic_slice_in_dim(modulated, first_col, columns, 1)
    return (summed_part.astype(jnp.bfloat16), modulated_part.astype(jnp.bfloat16))


def solution(mesh):
    return jax.shard_map(
        body,
        mesh=mesh,
        in_specs=(
            P("patch", None),
            P("patch", "tensor"),
            P("tensor"),
            P("patch", "tensor"),
            P("patch", "tensor"),
            P("tensor", None),
            P(),
            P(),
            P(),
            P(),
        ),
        out_specs=(P("patch", "tensor"), P("patch", "tensor")),
        check_vma=False,
    )
```

profile of v0, /device:TPU:1, one launch (start us, length us, event | category | flops | bytes accessed | tf_op | source)
XLA Modules:
  0.0 481.8 jit_solution(2331826031906205642)
XLA Ops:
  7.2 0.0 all-gather.3.cloned.1.call-start
  7.2 1.7 copy.15
  8.9 0.0 all-gather.3.cloned.1.call-update
  9.0 0.0 all-gather.5.cloned.1.call-start
  9.0 0.7 all-gather.5.cloned.1.call-update
  9.7 0.0 all-reduce.2.cloned.1.call-start
  9.8 1.1 copy.14
  10.8 0.1 fusion.15
  10.9 8.3 %psum.14 = f32[128]{0:T(128)S(1)} all-reduce(f32[128]{0:T(128)S(1)} %fusion.15), channel_id=1, replica_groups=mesh['patch'=64,'tensor'=4] {'tensor'}, use_global_device_ids=true, to_apply=%region_1.0 | all-reduce | flops 128 | bytes 1024 | tf_op jit(solution)/shard_map/psum | solution.py:26
  19.2 1.5 fusion.17
  20.7 185.3 %all-gather.3.cloned.1.call-done = bf16[8192,640]{0,1:T(8,128)(2,1)} async-done(((bf16[128,640]{0,1:T(8,128)(2,1)}), bf16[8192,640]{0,1:T(8,128)(2,1)}) %all-gather.3.cloned.1.call-update) | async-done | bytes 10485776 | tf_op jit(solution)/shard_map/all_gather | solution.py:32
  206.0 5.9 %multiply_reduce_fusion = (f32[5,128]{1,0:T(8,128)S(1)}, f32[5,128,8192]{2,1,0:T(8,128)S(1)}) fusion(bf16[128,5,128]{0,2,1:T(8,128)(2,1)} %bitcast.20, bf16[8192,5,128]{0,2,1:T(8,128)(2,1)} %bitcast.18), kind=kOutput, calls=%fused_computation.1 | convolution fusion | flops 1352662400 | bytes 31623680 | tf_op jit(solution)/shard_map/thc,jhc->htj/dot_general | solution.py:40
  212.0 0.0 copy-start
  212.0 7.0 %copy-done = f32[5,128,8192]{2,1,0:T(8,128)} copy-done((f32[5,128,8192]{2,1,0:T(8,128)}, f32[5,128,8192]{2,1,0:T(8,128)S(1)}, u32[]{:S(2)}) %copy-start) | copy-done | bytes 20971544
  219.0 4.2 fusion
  223.1 148.9 %all-gather.5.cloned.1.call-done = bf16[8192,640]{1,0:T(8,128)(2,1)} async-done(((bf16[128,640]{1,0:T(8,128)(2,1)}), bf16[8192,640]{1,0:T(8,128)(2,1)}) %all-gather.5.cloned.1.call-update) | async-done | bytes 10485776 | tf_op jit(solution)/shard_map/all_gather | solution.py:33
  372.0 0.0 slice-start
  372.0 14.6 %copy.18 = bf16[8192,640]{0,1:T(8,128)(2,1)} copy(bf16[8192,640]{1,0:T(8,128)(2,1)} %all-gather.5.cloned.1.call-done) | data formatting | bytes 20971520 | tf_op jit(solution)/shard_map/all_gather | solution.py:33
  386.7 0.0 slice-start.1
  386.7 12.4 %fusion.12 = bf16[128,5,128]{0,2,1:T(8,128)(2,1)S(1)} fusion(bf16[8192,5,128]{0,2,1:T(8,128)(2,1)} %bitcast.19, f32[5,128,8192]{2,1,0:T(8,128)} %copy-done, f32[5,128]{1,0:T(8,128)S(1)} %broadcast_maximum_fusion, f32[128,5]{0,1:T(8,128)S(1)} %bitcast.22), kind=kOutput, calls=%fused_computation.11 | convolution fusion | flops 1358069760 | bytes 31626240 | tf_op jit(solution)/shard_map/htj,jhc->htc/dot_general | solution.py:46
  399.1 0.0 copy-start.1
  399.1 0.0 copy-start.2
  399.1 0.0 copy-start.3
  399.1 0.0 slice-done
  399.1 0.0 slice-done.1
  399.1 2.8 fusion.20
  401.9 0.0 all-reduce.2.cloned.1.call-update
  401.9 0.0 copy-done.1
  401.9 0.1 dynamic-slice
  402.0 0.8 dynamic-slice.1
  402.8 67.9 %all-reduce.2.cloned.1.call-done = f32[128,5120]{1,0:T(8,128)} async-done(((f32[128,5120]{1,0:T(8,128)}), f32[128,5120]{1,0:T(8,128)}) %all-reduce.2.cloned.1.call-update) | async-done | bytes 2621456 | tf_op jit(solution)/shard_map/psum | solution.py:58
  470.7 0.0 copy-done.2
  470.7 0.0 copy-done.3
  470.7 2.9 fusion.19
  473.6 0.8 dynamic-slice_convert_fusion
  474.4 0.9 add_convert_fusion
  (5 shorter events, 0.0 us)
Async XLA Ops:
  7.2 198.9 %all-gather.3.cloned.1.call-start = ((), (), s32[]{:S(2)}) async-start(), calls=%async_computation | async-start | bytes 10649600 | tf_op jit(solution)/shard_map/all_gather | solution.py:32
  9.0 363.1 %all-gather.5.cloned.1.call-start = ((), (), s32[]{:S(2)}) async-start(), calls=%async_computation.1 | async-start | bytes 10649600 | tf_op jit(solution)/shard_map/all_gather | solution.py:33
  9.7 461.0 %all-reduce.2.cloned.1.call-start = ((), (), s32[]{:S(2)}) async-start(), calls=%async_computation.2 | async-start | bytes 5242880 | tf_op jit(solution)/shard_map/psum | solution.py:58
  212.0 7.0 %copy-start = (f32[5,128,8192]{2,1,0:T(8,128)}, f32[5,128,8192]{2,1,0:T(8,128)S(1)}, u32[]{:S(2)}) copy-start(f32[5,128,8192]{2,1,0:T(8,128)S(1)} %get-tuple-element.8) | copy-start | bytes 62914564
  372.0 27.1 %slice-start = ((s8[6553600]{0:T(1024)(128)(4,1)}), s8[2359296]{0:T(1024)(128)(4,1)S(1)}, s32[]{:S(2)}) async-start(s8[6553600]{0:T(1024)(128)(4,1)} %bitcast.16), calls=%async_computation.3 | async-start | bytes 4718592
  386.7 12.5 %slice-start.1 = ((s8[6553600]{0:T(1024)(128)(4,1)}), s8[4194304]{0:T(1024)(128)(4,1)S(1)}, s32[]{:S(2)}) async-start(s8[6553600]{0:T(1024)(128)(4,1)} %bitcast.16), calls=%async_computation.4 | async-start | bytes 8388608
  399.1 2.9 copy-start.1
  399.1 71.6 %copy-start.2 = (f32[5120]{0:T(1024)S(1)}, f32[5120]{0:T(1024)}, u32[]{:S(2)}) copy-start(f32[5120]{0:T(1024)} %param.16) | copy-start | bytes 61444
  399.1 71.6 %copy-start.3 = (f32[5120]{0:T(1024)S(1)}, f32[5120]{0:T(1024)}, u32[]{:S(2)}) copy-start(f32[5120]{0:T(1024)} %param.17) | copy-start | bytes 61444
Sparse Core Ops, SparseCore 0:
  12.0 194.0 all-gather.2
  209.5 162.4 all-gather.4
  402.0 68.6 all-reduce.1
where the time goes:
time: 482 us
  waiting for transfers between devices  403 us (84%)
  local copies, waits for them, and re-layouts  26.1 us (5%)
  matrix products  21.1 us (4%)
  between operations  13.9 us (3%)
  other arithmetic  9.64 us (2%)
  blocking collectives  8.25 us (2%)
    all_gather x1, waiting for transfers between devices, body(): lax.all_gather(stale_keys, 'patch', axis=0, tiled=True)  185 us
    all_gather x1, waiting for transfers between devices, body(): lax.all_gather(stale_values, 'patch', axis=0, tiled=True)  149 us
    psum x1, waiting for transfers between devices, body(): full_branch = lax.psum(partial_out, 'tensor')  67.9 us
    all_gather x1, local copies, waits for them, and re-layouts, body(): lax.all_gather(stale_values, 'patch', axis=0, tiled=True)  14.6 us
    dot_general x1, matrix products, body(): jnp.einsum('htj,jhc->htc', expo.astype(jnp.bfloat16), values_piece, prefe...  12.4 us
    unnamed x14, local copies, waits for them, and re-layouts  9.78 us
  transfers between devices with their start and end apart: 3, of which 3 were waited for; matrix products, arithmetic and copies ran while one was open for 3% of the time, Pallas kernels for 0%

commit v1 on v0

v1 whole, which is shorter than its diff:
```python
import functools
import math

import jax
import jax.numpy as jnp
from jax import lax
from jax.experimental import pallas as pl
from jax.experimental.pallas import tpu as pltpu
from jax.sharding import PartitionSpec as P

D = 5120
HEAD = 128
HD = 2560
ROWS = 128
NH = 5
NZ = 8
NG = 8
COLS = 1280
PART = 256
NP = COLS // PART
MESH = pl.DeviceIdType.MESH
SCALE = HEAD**-0.5 * math.log2(math.e)


def remote(src, dst, send, recv, device):
    return pltpu.make_async_remote_copy(
        src_ref=src, dst_ref=dst, send_sem=send, recv_sem=recv, device_id=device, device_id_type=MESH
    )


def lanes_of_rows(x):
    ones = jnp.ones((8, x.shape[1]), jnp.float32)
    return lax.dot_general(
        ones, x, (((1,), (1,)), ((), ())), precision=lax.Precision.HIGHEST, preferred_element_type=jnp.float32
    )


def kernel(
    query, gain, keys, values, hidden_hbm, weight_hbm, bias_hbm, gate_hbm, shift_hbm, norm_scale_hbm,
    residual, modulated,
    kbuf, vbuf, qbuf, osend, orecv, ssend, srecv, attended, weight, hidden, params,
    sq, stats, tosib, fromsib, tox, fromx, mine, summed,
    kv_send, kv_recv, q_send, q_recv, o_send, o_recv, s_send, s_recv, sq_send, sq_recv,
    st_send, st_recv, sib_send, sib_recv, x_send, x_recv, local,
):
    patch = lax.axis_index("patch")
    tensor = lax.axis_index("tensor")
    y, z, xh = patch // 16, (patch // 2) % 8, patch % 2
    xl, core = tensor // 2, tensor % 2
    group = y * 2 + xh

    def z_dev(step):
        return {"patch": y * 16 + ((z + step + NZ) % NZ) * 2 + xh, "tensor": tensor}

    def group_dev(r):
        g = (group + r) % NG
        return {"patch": (g // 2) * 16 + z * 2 + g % 2, "tensor": tensor}

    def tensor_dev(r):
        return {"patch": patch, "tensor": (tensor + r) % 4}

    sibling = {"patch": patch, "tensor": xl * 2 + (1 - core)}
    across = {"patch": patch, "tensor": (1 - xl) * 2 + core}

    barrier = pltpu.get_barrier_semaphore()
    for device in [z_dev(1), z_dev(-1)] + [group_dev(r) for r in range(1, NG)] + [tensor_dev(r) for r in range(1, 4)]:
        pl.semaphore_signal(barrier, inc=1, device_id=device, device_id_type=MESH)

    my_cols = pl.ds(pl.multiple_of(tensor * COLS, COLS), COLS)
    local_copies = [pltpu.make_async_copy(weight_hbm, weight, local.at[0])]
    local_copies.append(pltpu.make_async_copy(hidden_hbm.at[:, my_cols], hidden, local.at[1]))
    for i, ref in enumerate((bias_hbm, gate_hbm, shift_hbm, norm_scale_hbm)):
        local_copies.append(pltpu.make_async_copy(ref.at[:, my_cols], params.at[i], local.at[2 + i]))
    for copy in local_copies:
        copy.start()

    for h in range(NH):
        cols = slice(h * HEAD, (h + 1) * HEAD)
        kbuf[h, 0:ROWS, :] = keys[:, cols]
        vbuf[h, :, 0:ROWS] = jnp.transpose(values[:, cols].astype(jnp.float32)).astype(jnp.bfloat16)

    q32 = query[...].astype(jnp.float32)
    sq[0] = lanes_of_rows(q32 * q32)

    pl.semaphore_wait(barrier, 2 + NG - 1 + 3)

    def k_slot(h, d):
        return kbuf.at[h, pl.ds(d * ROWS, ROWS), :]

    def v_slot(h, d):
        return vbuf.at[h, :, pl.ds(d * ROWS, ROWS)]

    def hop(which, h, s, up):
        here = (NZ - s) % NZ if up else s
        there = NZ - s - 1 if up else s + 1
        slot = k_slot if which == 0 else v_slot
        return remote(
            slot(h, here), slot(h, there), kv_send.at[which, int(up), h, s], kv_recv.at[which, h, there],
            z_dev(1 if up else -1),
        )

    def hops(s):
        if s < 3:
            return [(0, True), (1, True), (0, False), (1, False)]
        return [(0, True), (1, False)]

    def arrived(which, h, d):
        slot = k_slot if which == 0 else v_slot
        remote(slot(h, d), slot(h, d), kv_send.at[0, 0, 0, 0], kv_recv.at[which, h, d], z_dev(1)).wait_recv()

    def pass_on(h, s):
        for up in (True, False):
            for which in (0, 1):
                if s > 0:
                    arrived(which, h, NZ - s if up else s)
                if (which, up) in hops(s):
                    hop(which, h, s, up).start()

    pass_on(0, 0)

    def sq_copy(r):
        return remote(sq.at[0], sq.at[4 - r], sq_send.at[r], sq_recv.at[4 - r], tensor_dev(r))

    for r in range(1, 4):
        sq_copy(r).start()
    for h in range(1, NH):
        pass_on(h, 0)
    for r in range(1, 4):
        sq_copy(4 - r).wait_recv()
    squares = sq[0] + sq[1] + sq[2] + sq[3]
    factor = lax.rsqrt(squares / HD + 1e-06) * SCALE
    factor = jnp.transpose(factor)[:, 0:1]
    normed = (q32 * factor * gain[...]).astype(jnp.bfloat16)
    for h in range(NH):
        qbuf[h, 0:ROWS, :] = normed[:, h * HEAD : (h + 1) * HEAD]

    def q_copy(h, r):
        return remote(
            qbuf.at[h, pl.ds(0, ROWS), :], qbuf.at[h, pl.ds((NG - r) * ROWS, ROWS), :],
            q_send.at[h, r], q_recv.at[h, NG - r], group_dev(r),
        )

    def send_queries(h, carry):
        for r in range(1, NG):
            q_copy(h, r).start()
        return carry

    lax.fori_loop(0, NH, send_queries, 0)

    def o_copy(h, r):
        return remote(osend.at[h, r], orecv.at[h, NG - r], o_send.at[h, r], o_recv.at[h, NG - r], group_dev(r))

    def s_copy(h, r):
        return remote(ssend.at[h, r], srecv.at[h, NG - r], s_send.at[h, r], s_recv.at[h, NG - r], group_dev(r))

    def attend(h, j):
        for r in (2 * j, 2 * j + 1):
            if r > 0:
                q_copy(h, NG - r).wait_recv()
        q = qbuf[h, 2 * j * ROWS : (2 * j + 2) * ROWS, :]
        scores = lax.dot_general(kbuf[h], q, (((1,), (1,)), ((), ())), preferred_element_type=jnp.float32)
        top = jnp.max(scores, axis=0, keepdims=True)
        expo = jnp.exp2(scores - top)
        total = jnp.sum(expo, axis=0, keepdims=True)
        mixed = jnp.dot(vbuf[h], expo.astype(jnp.bfloat16), preferred_element_type=jnp.float32)
        for r in (2 * j, 2 * j + 1):
            part = slice((r - 2 * j) * ROWS, (r - 2 * j + 1) * ROWS)
            o_ref, s_ref = (osend, ssend) if r > 0 else (orecv, srecv)
            o_ref[h, r] = mixed[:, part].astype(jnp.bfloat16)
            s_ref[h, r, 0:1, :] = top[:, part]
            s_ref[h, r, 1:2, :] = total[:, part]
            if r > 0:
                o_copy(h, r).start()
                s_copy(h, r).start()

    def combine(h):
        for r in range(1, NG):
            o_copy(h, NG - r).wait_recv()
            s_copy(h, NG - r).wait_recv()
        top = srecv[h, 0, 0:1, :]
        for r in range(1, NG):
            top = jnp.maximum(top, srecv[h, r, 0:1, :])
        num = jnp.zeros((HEAD, ROWS), jnp.float32)
        den = jnp.zeros((1, ROWS), jnp.float32)
        for r in range(NG):
            share = jnp.exp2(srecv[h, r, 0:1, :] - top)
            den = den + share * srecv[h, r, 1:2, :]
            num = num + share * orecv[h, r].astype(jnp.float32)
        attended[:, pl.ds(pl.multiple_of(h * HEAD, HEAD), HEAD)] = jnp.transpose(num / den).astype(jnp.bfloat16)

    def turn(tau, carry):
        for i in range(4):
            if i < 3:
                s = i + 1
                h = tau - i

                @pl.when((h >= 0) & (h < NH))
                def _(h=h, s=s):
                    pass_on(h, s)

            @pl.when((tau >= 3) & (tau < 3 + NH))
            def _(h=tau - 3, i=i):
                if i == 0:
                    arrived(0, h, 4)
                    arrived(1, h, 4)
                attend(h, (i + 1) % 4)

        @pl.when(tau >= 4)
        def _(h=tau - 4):
            combine(h)

        return carry

    lax.fori_loop(0, 4 + NH, turn, 0)

    for copy in local_copies:
        copy.wait()

    def project(block, part):
        cols = pl.ds(pl.multiple_of(block * COLS + part * PART, PART), PART)
        return jnp.dot(attended[...], weight[:, cols], preferred_element_type=jnp.float32)

    def sib_copy(i, part):
        return remote(tosib.at[i, part], fromsib.at[i, part], sib_send.at[i, part], sib_recv.at[i, part], sibling)

    def x_copy(part):
        return remote(tox.at[part], fromx.at[part], x_send.at[part], x_recv.at[part], across)

    def stage(i, block):
        def step(part, carry):
            tosib[i, part] = project(block, part).astype(jnp.bfloat16)
            sib_copy(i, part).start()
            return carry

        lax.fori_loop(0, NP, step, 0)

    stage(0, (1 - xl) * 2 + (1 - core))

    def step_across(part, carry):
        ours = project((1 - xl) * 2 + core, part)
        sib_copy(0, part).wait_recv()
        tox[part] = (ours + fromsib[0, part].astype(jnp.float32)).astype(jnp.bfloat16)
        x_copy(part).start()
        return carry

    lax.fori_loop(0, NP, step_across, 0)
    stage(1, xl * 2 + (1 - core))

    def step_mine(part, carry):
        mine[part] = project(tensor, part)
        return carry

    lax.fori_loop(0, NP, step_mine, 0)

    total = jnp.zeros((ROWS, HEAD), jnp.float32)
    total_sq = jnp.zeros((ROWS, HEAD), jnp.float32)
    for part in range(NP):
        cols = slice(part * PART, (part + 1) * PART)
        sib_copy(1, part).wait_recv()
        x_copy(part).wait_recv()
        branch = mine[part] + fromsib[1, part].astype(jnp.float32) + fromx[part].astype(jnp.float32)
        branch = branch + params[0, :, cols]
        value = hidden[:, cols].astype(jnp.float32) + params[1, :, cols] * branch
        summed[:, cols] = value
        residual[:, cols] = value.astype(jnp.bfloat16)
        for lo in range(0, PART, HEAD):
            piece = value[:, lo : lo + HEAD]
            total = total + piece
            total_sq = total_sq + piece * piece
    stats[0, 0] = lanes_of_rows(total)
    stats[0, 1] = lanes_of_rows(total_sq)

    def st_copy(r):
        return remote(stats.at[0], stats.at[4 - r], st_send.at[r], st_recv.at[4 - r], tensor_dev(r))

    for r in range(1, 4):
        st_copy(r).start()
    for r in range(1, 4):
        st_copy(4 - r).wait_recv()
    mean = (stats[0, 0] + stats[1, 0] + stats[2, 0] + stats[3, 0]) / D
    var = (stats[0, 1] + stats[1, 1] + stats[2, 1] + stats[3, 1]) / D - mean * mean
    inv = lax.rsqrt(var + 1e-06)
    mean = jnp.transpose(mean)[:, 0:1]
    inv = jnp.transpose(inv)[:, 0:1]
    for part in range(NP):
        cols = slice(part * PART, (part + 1) * PART)
        value = (summed[:, cols] - mean) * inv * (1.0 + params[3, :, cols]) + params[2, :, cols]
        modulated[:, cols] = value.astype(jnp.bfloat16)

    def drain(h, carry):
        for s in range(4):
            for which, up in hops(s):
                hop(which, h, s, up).wait_send()
        for r in range(1, NG):
            q_copy(h, r).wait_send()
            o_copy(h, r).wait_send()
            s_copy(h, r).wait_send()
        return carry

    lax.fori_loop(0, NH, drain, 0)
    for r in range(1, 4):
        sq_copy(r).wait_send()
        st_copy(r).wait_send()

    def drain_parts(part, carry):
        sib_copy(0, part).wait_send()
        sib_copy(1, part).wait_send()
        x_copy(part).wait_send()
        return carry

    lax.fori_loop(0, NP, drain_parts, 0)


def body(
    hidden, query, query_gain, stale_keys, stale_values, out_weight, out_bias, residual_gate, norm_shift, norm_scale
):
    bf16, f32 = jnp.bfloat16, jnp.float32
    vmem = pl.BlockSpec(memory_space=pltpu.VMEM)
    hbm = pl.BlockSpec(memory_space=pl.ANY)
    dma = pltpu.SemaphoreType.DMA
    row = lambda x: x.reshape(1, -1)
    out = jax.ShapeDtypeStruct((ROWS, COLS), bf16)
    return pl.pallas_call(
        kernel,
        out_shape=(out, out),
        in_specs=[vmem] * 4 + [hbm] * 6,
        out_specs=(vmem, vmem),
        scratch_shapes=[
            pltpu.VMEM((NH, NZ * ROWS, HEAD), bf16),
            pltpu.VMEM((NH, HEAD, NZ * ROWS), bf16),
            pltpu.VMEM((NH, NG * ROWS, HEAD), bf16),
            pltpu.VMEM((NH, NG, HEAD, ROWS), bf16),
            pltpu.VMEM((NH, NG, HEAD, ROWS), bf16),
            pltpu.VMEM((NH, NG, 8, ROWS), f32),
            pltpu.VMEM((NH, NG, 8, ROWS), f32),
            pltpu.VMEM((ROWS, NH * HEAD), bf16),
            pltpu.VMEM((NH * HEAD, D), bf16),
            pltpu.VMEM((ROWS, COLS), bf16),
            pltpu.VMEM((4, 1, COLS), f32),
            pltpu.VMEM((4, 8, ROWS), f32),
            pltpu.VMEM((4, 2, 8, ROWS), f32),
            pltpu.VMEM((2, NP, ROWS, PART), bf16),
            pltpu.VMEM((2, NP, ROWS, PART), bf16),
            pltpu.VMEM((NP, ROWS, PART), bf16),
            pltpu.VMEM((NP, ROWS, PART), bf16),
            pltpu.VMEM((NP, ROWS, PART), f32),
            pltpu.VMEM((ROWS, COLS), f32),
            dma((2, 2, NH, 4)),
            dma((2, NH, NZ)),
            dma((NH, NG)),
            dma((NH, NG)),
            dma((NH, NG)),
            dma((NH, NG)),
            dma((NH, NG)),
            dma((NH, NG)),
            dma((4,)),
            dma((4,)),
            dma((4,)),
            dma((4,)),
            dma((2, NP)),
            dma((2, NP)),
            dma((NP,)),
            dma((NP,)),
            dma((6,)),
        ],
        compiler_params=pltpu.CompilerParams(
            collective_id=0, has_side_effects=True, vmem_limit_bytes=48 * 2**20
        ),
        name="attention_block",
    )(
        query, row(query_gain), stale_keys, stale_values, hidden, out_weight,
        row(out_bias), row(residual_gate), row(norm_shift), row(norm_scale),
    )


def solution(mesh):
    return jax.shard_map(
        body,
        mesh=mesh,
        in_specs=(
            P("patch", None),
            P("patch", "tensor"),
            P("tensor"),
            P("patch", "tensor"),
            P("patch", "tensor"),
            P("tensor", None),
            P(),
            P(),
            P(),
            P(),
        ),
        out_specs=(P("patch", "tensor"), P("patch", "tensor")),
        check_vma=False,
    )
```

time: 482 us -> 86.2 us (0.18)
  waiting for transfers between devices: 403 us -> 0 us
  Pallas kernels: 0 us -> 76 us
  matrix products: 21.1 us -> 0 us
  local copies, waits for them, and re-layouts: 26.1 us -> 9.11 us
  between operations: 13.9 us -> 0.65 us
  other arithmetic: 9.64 us -> 0 us
  blocking collectives: 8.25 us -> 0 us
    all_gather x2 -> x0, waiting for transfers between devices: 334 us -> none  [the longest x1 185 us: body(): lax.all_gather(stale_keys, 'patch', axis=0, tiled=True)]
    pallas_call x0 -> x1, Pallas kernels: none -> 76 us  [body(): pl.pallas_call(kernel, out_shape=(out, out), in_specs=[vmem] * 4 + [hbm]...]
    psum x1 -> x0, waiting for transfers between devices: 67.9 us -> none  [body(): full_branch = lax.psum(partial_out, 'tensor')]
    dot_general x3 -> x0, matrix products: 21.1 us -> none  [the longest x1 12.4 us: body(): jnp.einsum('htj,jhc->htc', expo.astype(jnp.bfloat16), values_piece, prefe...]
    all_gather x1 -> x0, local copies, waits for them, and re-layouts: 14.6 us -> none  [body(): lax.all_gather(stale_values, 'patch', axis=0, tiled=True)]
    psum x1 -> x0, blocking collectives: 8.25 us -> none  [body(): squares = lax.psum(jnp.sum(query_wide * query_wide, axis=1), 'tensor')]
    reduce_sum x3 -> x0, other arithmetic: 7.18 us -> none  [the longest x1 4.17 us: body(): totals = jnp.sum(expo, axis=2)]
    unnamed x14 -> x18, local copies, waits for them, and re-layouts: 9.78 us -> 8.42 us
  transfers between devices with their start and end apart: 3 -> 0, of which waited for: 3 -> 0; matrix products, arithmetic and copies ran while one was open for 3% -> 0% of each run, Pallas kernels for 0% -> 0%
where the time goes in v1:
time: 86.2 us; the launch traced here: 85.8 us
  Pallas kernels  76 us (88%)
  local copies, waits for them, and re-layouts  9.11 us (11%)
    pallas_call x1, Pallas kernels, body(): pl.pallas_call(kernel, out_shape=(out, out), in_specs=[vmem] * 4 + [hbm]...  76 us
    unnamed x18, local copies, waits for them, and re-layouts  8.42 us

profile of v1, /device:TPU:1, one launch (start us, length us, event | category | flops | bytes accessed | tf_op | source)
XLA Modules:
  0.0 85.8 jit_solution(18076893326473270116)
XLA Ops:
  0.6 0.7 reshape.19.gain
  1.3 0.0 copy-start
  1.3 1.3 %copy-done = bf16[128,5120]{1,0:T(8,128)(2,1)S(1)} copy-done((bf16[128,5120]{1,0:T(8,128)(2,1)S(1)}, bf16[128,5120]{1,0:T(8,128)(2,1)}, u32[]{:S(2)}) %copy-start) | copy-done | bytes 1310744
  2.6 0.0 copy-start.1
  2.6 0.9 %copy-done.1 = bf16[128,640]{1,0:T(8,128)(2,1)S(1)} copy-done((bf16[128,640]{1,0:T(8,128)(2,1)S(1)}, bf16[128,640]{1,0:T(8,128)(2,1)}, u32[]{:S(2)}) %copy-start.1) | copy-done | bytes 163864
  3.6 0.0 copy-start.2
  3.6 0.9 %copy-done.2 = bf16[128,640]{1,0:T(8,128)(2,1)S(1)} copy-done((bf16[128,640]{1,0:T(8,128)(2,1)S(1)}, bf16[128,640]{1,0:T(8,128)(2,1)}, u32[]{:S(2)}) %copy-start.2) | copy-done | bytes 163864
  4.5 0.0 copy-start.3
  4.5 0.9 %copy-done.3 = bf16[128,640]{1,0:T(8,128)(2,1)S(1)} copy-done((bf16[128,640]{1,0:T(8,128)(2,1)S(1)}, bf16[128,640]{1,0:T(8,128)(2,1)}, u32[]{:S(2)}) %copy-start.3) | copy-done | bytes 163864
  5.4 0.0 copy-start.4
  5.4 0.7 copy-done.4
  6.1 0.0 copy-start.5
  6.1 0.7 copy-done.5
  6.8 0.0 copy-start.6
  6.8 0.7 copy-done.6
  7.6 0.0 copy-start.7
  7.6 0.7 copy-done.7
  8.3 76.0 %attention_block.1 = (bf16[128,1280]{1,0:T(8,128)(2,1)S(1)}, bf16[128,1280]{1,0:T(8,128)(2,1)S(1)}) custom-call(bf16[128,640]{1,0:T(8,128)(2,1)S(1)} %copy-done.1, f32[1,640]{1,0:T(1,128)S(1)} %reshape.19.gain, bf16[128,640]{1,0:T(8,128)(2,1)S(1)} %copy-done.2, bf16[128,640]{1,0:T(8,128)(2,1)S(1)} %copy-done.3, bf16[128,5120]{1,0:T(8,128)(2,1)S(1)} %copy-done, ...), custom_call_target="tpu_custom_call" | custom-call | tf_op jit(solution)/shard_map/attention_block/pallas_call | solution.py:323
  84.3 0.7 copy.14
  85.1 0.7 copy.15
Async XLA Ops:
  1.3 1.3 %copy-start = (bf16[128,5120]{1,0:T(8,128)(2,1)S(1)}, bf16[128,5120]{1,0:T(8,128)(2,1)}, u32[]{:S(2)}) copy-start(bf16[128,5120]{1,0:T(8,128)(2,1)} %hidden_hbm.1) | copy-start | bytes 3932164
  2.6 0.9 %copy-start.1 = (bf16[128,640]{1,0:T(8,128)(2,1)S(1)}, bf16[128,640]{1,0:T(8,128)(2,1)}, u32[]{:S(2)}) copy-start(bf16[128,640]{1,0:T(8,128)(2,1)} %query.1) | copy-start | bytes 491524
  3.6 0.9 %copy-start.2 = (bf16[128,640]{1,0:T(8,128)(2,1)S(1)}, bf16[128,640]{1,0:T(8,128)(2,1)}, u32[]{:S(2)}) copy-start(bf16[128,640]{1,0:T(8,128)(2,1)} %keys.1) | copy-start | bytes 491524
  4.5 0.9 %copy-start.3 = (bf16[128,640]{1,0:T(8,128)(2,1)S(1)}, bf16[128,640]{1,0:T(8,128)(2,1)}, u32[]{:S(2)}) copy-start(bf16[128,640]{1,0:T(8,128)(2,1)} %values.1) | copy-start | bytes 491524
  5.4 0.7 copy-start.4
  6.1 0.7 copy-start.5
  6.8 0.7 copy-start.6
  7.6 0.7 copy-start.7

commit v2 on v0

v2 whole, which is shorter than its diff:
```python
import functools
import math

import jax
import jax.numpy as jnp
from jax import lax
from jax.experimental import pallas as pl
from jax.experimental.pallas import tpu as pltpu
from jax.sharding import PartitionSpec as P

D = 5120
HEAD = 128
HD = 2560
ROWS = 128
NH = 5
GROUPS = ((0, 2), (2, 2), (4, 1))
NG = len(GROUPS)
NZ = 8
NY = 4
NEAR = 5
COLS = 1280
PART = 256
NP = COLS // PART
MESH = pl.DeviceIdType.MESH
SCALE = HEAD**-0.5 * math.log2(math.e)
CONTRACT_LAST = (((1,), (1,)), ((), ()))


def remote(src, dst, send, recv, device):
    return pltpu.make_async_remote_copy(
        src_ref=src, dst_ref=dst, send_sem=send, recv_sem=recv, device_id=device, device_id_type=MESH
    )


def columns_to_rows(first, second):
    n = first.shape[0]
    lane = lax.broadcasted_iota(jnp.int32, (n, HEAD), 1)
    return jnp.transpose(jnp.where(lane == 0, first, second))[0:8]


def kernel(
    query_hbm, gain_hbm, keys_hbm, values_hbm, hidden_hbm, weight_hbm, bias_hbm, gate_hbm, shift_hbm, norm_scale_hbm,
    residual, modulated,
    query, gain, keys, values, weight, hidden, params,
    kvstage, qstage, kv, qbuf, osend, orecv, ssend, srecv, near_mix, near_top, near_total, attended, acc,
    sq, stats, tosib, fromsib, tox, fromx, mine, summed,
    swap_send, kv_send, kv_recv, pair_send, pair_recv, q_send, q_recv, o_send, o_recv, s_send, s_recv, sq_send, sq_recv,
    st_send, st_recv, sib_send, sib_recv, x_send, x_recv, local,
):
    patch = lax.axis_index("patch")
    tensor = lax.axis_index("tensor")
    y, z, xh = patch // 16, (patch // 2) % 8, patch % 2
    xl, core = tensor // 2, tensor % 2
    straight = xh == core

    def z_dev(step):
        return {"patch": y * 16 + ((z + step + NZ) % NZ) * 2 + xh, "tensor": tensor}

    def group_dev(r):
        return {"patch": ((y + r) % NY) * 16 + z * 2 + core, "tensor": xl * 2 + xh}

    def tensor_dev(r):
        return {"patch": patch, "tensor": (tensor + r) % 4}

    sibling = {"patch": patch, "tensor": xl * 2 + (1 - core)}
    across = {"patch": patch, "tensor": (1 - xl) * 2 + core}

    barrier = pltpu.get_barrier_semaphore()
    partners = [z_dev(1), z_dev(-1)] + [group_dev(r) for r in range(1, NY)] + [tensor_dev(r) for r in range(1, 4)]
    for device in partners:
        pl.semaphore_signal(barrier, inc=1, device_id=device, device_id_type=MESH)

    @pl.when(jnp.logical_not(straight))
    def _():
        pl.semaphore_signal(barrier, inc=1, device_id=group_dev(0), device_id_type=MESH)

    my_cols = pl.ds(pl.multiple_of(tensor * COLS, COLS), COLS)
    early = [(keys_hbm, keys), (values_hbm, values), (query_hbm, query), (gain_hbm, gain)]
    late = [(weight_hbm, weight), (hidden_hbm.at[:, my_cols], hidden)]
    late += [(ref.at[:, my_cols], params.at[i]) for i, ref in enumerate((bias_hbm, gate_hbm, shift_hbm, norm_scale_hbm))]
    copies = [pltpu.make_async_copy(src, dst, local.at[i]) for i, (src, dst) in enumerate(early + late)]
    for copy in copies:
        copy.start()

    copies[0].wait()
    copies[1].wait()
    for h in range(NH):
        cols = slice(h * HEAD, (h + 1) * HEAD)
        kvstage[h, 0:ROWS, :] = keys[:, cols]
        kvstage[h, ROWS:, :] = values[:, cols]

    copies[2].wait()
    copies[3].wait()
    q32 = query[...].astype(jnp.float32)
    squares = jnp.sum(q32 * q32, axis=1, keepdims=True)
    sq[0] = columns_to_rows(squares, squares)

    @pl.when(straight)
    def _():
        pl.semaphore_wait(barrier, len(partners))

    @pl.when(jnp.logical_not(straight))
    def _():
        pl.semaphore_wait(barrier, len(partners) + 1)

    def to_group(src, dst, send, recv, r, wait=False):
        copy = remote(src, dst, send, recv, group_dev(r))
        act = copy.wait_send if wait else copy.start
        if r > 0:
            act()
            return
        pl.when(jnp.logical_not(straight))(act)
        if not wait:
            pl.when(straight)(pltpu.make_async_copy(src, dst, recv).start)

    def landed(ref, recv):
        remote(ref, ref, swap_send.at[0], recv, z_dev(1)).wait_recv()

    def heads(g):
        return pl.ds(*GROUPS[g])

    def swap(g, wait=False):
        to_group(kvstage.at[heads(g)], kv.at[0, 0, heads(g)], swap_send.at[g], kv_recv.at[g, 0], 0, wait)

    def place(s, up):
        return 0 if s == 0 else 2 * s - 1 if up or s == 4 else 2 * s

    def block(g, s, up):
        if s == 4:
            return kv.at[7, 0, heads(g), pl.ds(0 if up else ROWS, ROWS)]
        return kv.at[place(s, up), 0, heads(g)]

    def block_sem(g, s, up):
        return kv_recv.at[g, 8 if s == 4 and not up else place(s, up)]

    def hop(g, s, up):
        src = block(g, s, up)
        if s == 3:
            src = kv.at[place(s, up), 0, heads(g), pl.ds(0 if up else ROWS, ROWS)]
        return remote(
            src, block(g, s + 1, up), kv_send.at[g, int(up), s], block_sem(g, s + 1, up), z_dev(1 if up else -1)
        )

    shares = ((0, 1), (1, 2), (3, 2), (5, 3))

    def pair(g, m):
        places = pl.ds(*shares[m])
        return remote(
            kv.at[places, 0, heads(g)], kv.at[places, 1, heads(g)], pair_send.at[g, m], pair_recv.at[g, m], sibling
        )

    def event(g, s):
        if s == 0:
            landed(block(g, 0, True), block_sem(g, 0, True))
        for up in (True, False):
            if s > 0:
                landed(block(g, s, up), block_sem(g, s, up))
            if s < 4:
                hop(g, s, up).start()
        if s != 3:
            pair(g, min(s, 3)).start()

    for g in range(NG):
        swap(g)

    def sq_copy(r):
        return remote(sq.at[0], sq.at[4 - r], sq_send.at[r], sq_recv.at[4 - r], tensor_dev(r))

    for r in range(1, 4):
        sq_copy(r).start()
    event(0, 0)
    event(1, 0)
    for r in range(1, 4):
        sq_copy(4 - r).wait_recv()
    factor = lax.rsqrt((sq[0] + sq[1] + sq[2] + sq[3]) / HD + 1e-06) * SCALE
    factor = jnp.transpose(factor)[:, 0:1]
    normed = (q32 * factor * gain[...][None, :]).astype(jnp.bfloat16)
    for h in range(NH):
        qstage[h] = normed[:, h * HEAD : (h + 1) * HEAD]

    def send_query(r, wait=False):
        back = (NY - r) % NY
        to_group(qstage, qbuf.at[back], q_send.at[r], q_recv.at[back], r, wait)

    for r in range(NY):
        send_query(r)
    event(2, 0)
    event(0, 1)
    event(1, 1)
    for r in range(NY):
        landed(qbuf.at[r], q_recv.at[r])
    event(0, 2)

    def send_mixed(g, r, wait=False):
        back = (NY - r) % NY
        to_group(osend.at[r, heads(g)], orecv.at[back, heads(g)], o_send.at[g, r], o_recv.at[g, back], r, wait)
        to_group(ssend.at[r, heads(g)], srecv.at[back, heads(g)], s_send.at[g, r], s_recv.at[g, back], r, wait)

    def scores_of(h, j, first, count):
        q = qbuf[pl.ds(2 * j, 2), h].reshape(2 * ROWS, HEAD)
        k = kv[first : first + count, :, h, 0:ROWS, :].reshape(count * 2 * ROWS, HEAD)
        return lax.dot_general(q, k, CONTRACT_LAST, preferred_element_type=jnp.float32)

    def mix(h, expo, first, count):
        v = kv[first : first + count, :, h, ROWS : 2 * ROWS, :].reshape(count * 2 * ROWS, HEAD)
        return jnp.dot(expo.astype(jnp.bfloat16), v, preferred_element_type=jnp.float32)

    def attend_near(h, j):
        scores = scores_of(h, j, 0, NEAR)
        top = jnp.max(scores, axis=1, keepdims=True)
        expo = jnp.exp2(scores - top)
        near_top[h, j] = top
        near_total[h, j] = jnp.sum(expo, axis=1, keepdims=True)
        near_mix[h, j] = mix(h, expo, 0, NEAR)

    def attend_far(h, j):
        scores = scores_of(h, j, NEAR, NZ - NEAR)
        top = jnp.maximum(near_top[h, j], jnp.max(scores, axis=1, keepdims=True))
        expo = jnp.exp2(scores - top)
        fade = jnp.exp2(near_top[h, j] - top)
        total = near_total[h, j] * fade + jnp.sum(expo, axis=1, keepdims=True)
        mixed = (near_mix[h, j] * fade + mix(h, expo, NEAR, NZ - NEAR)).astype(jnp.bfloat16)
        numbers = columns_to_rows(top, total)
        for i in range(2):
            part = slice(i * ROWS, (i + 1) * ROWS)
            osend[2 * j + i, h] = mixed[part]
            ssend[2 * j + i, h] = numbers[:, part]

    def near(g, between=None):
        for m in range(3):
            pair(g, m).wait_recv()
        first, count = GROUPS[g]

        def step(i, carry):
            attend_near(first + i % count, 1 - i // count)
            return carry

        lax.fori_loop(0, 2 * count, step, 0)

    def far(g):
        pair(g, 3).wait_recv()
        first, count = GROUPS[g]

        def step(i, carry):
            attend_far(first + i % count, 1 - i // count)
            for j in (1, 0):

                @pl.when(i == (2 - j) * count - 1)
                def _(j=j):
                    send_mixed(g, 2 * j + 1)
                    send_mixed(g, 2 * j)

            return carry

        lax.fori_loop(0, 2 * count, step, 0)

    def combine(g):
        for r in range(NY):
            landed(orecv.at[r, heads(g)], o_recv.at[g, r])
            landed(srecv.at[r, heads(g)], s_recv.at[g, r])
        first, count = GROUPS[g]
        for h in range(first, first + count):
            numbers = jnp.transpose(jnp.concatenate([srecv[r, h] for r in range(NY)], axis=0))
            tops = [numbers[:, 8 * r : 8 * r + 1] for r in range(NY)]
            top = functools.reduce(jnp.maximum, tops)
            shares = [jnp.exp2(t - top) for t in tops]
            den = sum(shares[r] * numbers[:, 8 * r + 1 : 8 * r + 2] for r in range(NY))
            num = sum(shares[r] * orecv[r, h].astype(jnp.float32) for r in range(NY))
            attended[:, h * HEAD : (h + 1) * HEAD] = (num / den).astype(jnp.bfloat16)

    def project(g, columns):
        first, count = GROUPS[g]
        rows = slice(first * HEAD, (first + count) * HEAD)
        return jnp.dot(attended[:, rows], weight[rows, columns], preferred_element_type=jnp.float32)

    def project_early(g):
        def step(b, carry):
            part = project(g, pl.ds(pl.multiple_of(b * COLS, COLS), COLS))
            acc[b] = part if g == 0 else acc[b] + part
            return carry

        lax.fori_loop(0, 4, step, 0)

    event(2, 1)
    event(1, 2)
    near(0)
    event(0, 3)
    event(1, 3)
    event(2, 2)
    event(0, 4)
    near(1)
    event(2, 3)
    event(1, 4)
    far(0)
    near(2)
    event(2, 4)
    far(1)
    copies[4].wait()
    combine(0)
    far(2)
    project_early(0)
    combine(1)
    project_early(1)
    combine(2)

    for copy in copies[5:]:
        copy.wait()

    def branch_part(b, part):
        cols = pl.ds(pl.multiple_of(b * COLS + part * PART, PART), PART)
        return acc[b, :, part * PART : (part + 1) * PART] + project(NG - 1, cols)

    def sib_copy(i, part):
        return remote(tosib.at[i, part], fromsib.at[i, part], sib_send.at[i, part], sib_recv.at[i, part], sibling)

    def x_copy(part):
        return remote(tox.at[part], fromx.at[part], x_send.at[part], x_recv.at[part], across)

    def stage(i, b):
        for part in range(NP):
            tosib[i, part] = branch_part(b, part).astype(jnp.bfloat16)
            sib_copy(i, part).start()

    stage(0, (1 - xl) * 2 + (1 - core))
    for part in range(NP):
        ours = branch_part((1 - xl) * 2 + core, part)
        sib_copy(0, part).wait_recv()
        tox[part] = (ours + fromsib[0, part].astype(jnp.float32)).astype(jnp.bfloat16)
        x_copy(part).start()
    stage(1, xl * 2 + (1 - core))
    for part in range(NP):
        cols = slice(part * PART, (part + 1) * PART)
        branch = branch_part(tensor, part) + params[0, :, cols]
        sib_copy(1, part).wait_recv()
        mine[part] = hidden[:, cols].astype(jnp.float32) + params[1, :, cols] * (
            branch + fromsib[1, part].astype(jnp.float32)
        )

    total = jnp.zeros((ROWS, HEAD), jnp.float32)
    total_sq = jnp.zeros((ROWS, HEAD), jnp.float32)
    for part in range(NP):
        cols = slice(part * PART, (part + 1) * PART)
        x_copy(part).wait_recv()
        value = mine[part] + params[1, :, cols] * fromx[part].astype(jnp.float32)
        summed[:, cols] = value
        residual[:, cols] = value.astype(jnp.bfloat16)
        for lo in range(0, PART, HEAD):
            piece = value[:, lo : lo + HEAD]
            total = total + piece
            total_sq = total_sq + piece * piece
    stats[0] = columns_to_rows(
        jnp.sum(total, axis=1, keepdims=True), jnp.sum(total_sq, axis=1, keepdims=True)
    )

    def st_copy(r):
        return remote(stats.at[0], stats.at[4 - r], st_send.at[r], st_recv.at[4 - r], tensor_dev(r))

    for r in range(1, 4):
        st_copy(r).start()

    for g in range(NG):
        swap(g, wait=True)
        for up in (True, False):
            for s in range(4):
                hop(g, s, up).wait_send()
        for m in range(len(shares)):
            pair(g, m).wait_send()
        for r in range(NY):
            send_mixed(g, r, wait=True)
    for r in range(NY):
        send_query(r, wait=True)
    for r in range(1, 4):
        sq_copy(r).wait_send()
    for part in range(NP):
        sib_copy(0, part).wait_send()
        sib_copy(1, part).wait_send()
        x_copy(part).wait_send()

    for r in range(1, 4):
        st_copy(4 - r).wait_recv()
    both = jnp.transpose(stats[0] + stats[1] + stats[2] + stats[3]) / D
    mean = both[:, 0:1]
    inv = lax.rsqrt(both[:, 1:2] - mean * mean + 1e-06)
    for part in range(NP):
        cols = slice(part * PART, (part + 1) * PART)
        value = (summed[:, cols] - mean) * inv * (1.0 + params[3, :, cols]) + params[2, :, cols]
        modulated[:, cols] = value.astype(jnp.bfloat16)
    for r in range(1, 4):
        st_copy(r).wait_send()


def deliver(first_in, second_in, first_out, second_out, sems):
    half = ROWS // 2
    copies = [
        pltpu.make_async_copy(src.at[pl.ds(i * half, half)], dst.at[pl.ds(i * half, half)], sems.at[2 * k + i])
        for k, (src, dst) in enumerate(((first_in, first_out), (second_in, second_out)))
        for i in range(2)
    ]
    for copy in copies:
        copy.start()
    for copy in copies:
        copy.wait()


def body(
    hidden, query, query_gain, stale_keys, stale_values, out_weight, out_bias, residual_gate, norm_shift, norm_scale
):
    bf16, f32 = jnp.bfloat16, jnp.float32
    vmem = pl.BlockSpec(memory_space=pltpu.VMEM)
    hbm = pl.BlockSpec(memory_space=pltpu.HBM)
    dma = pltpu.SemaphoreType.DMA
    row = lambda x: x.reshape(1, -1)
    out = jax.ShapeDtypeStruct((ROWS, COLS), bf16)
    results = pl.pallas_call(
        kernel,
        out_shape=(out, out),
        in_specs=[hbm] * 10,
        out_specs=(vmem, vmem),
        scratch_shapes=[
            pltpu.VMEM((ROWS, NH * HEAD), bf16),
            pltpu.VMEM((NH * HEAD,), f32),
            pltpu.VMEM((ROWS, NH * HEAD), bf16),
            pltpu.VMEM((ROWS, NH * HEAD), bf16),
            pltpu.VMEM((NH * HEAD, D), bf16),
            pltpu.VMEM((ROWS, COLS), bf16),
            pltpu.VMEM((4, 1, COLS), f32),
            pltpu.VMEM((NH, 2 * ROWS, HEAD), bf16),
            pltpu.VMEM((NH, ROWS, HEAD), bf16),
            pltpu.VMEM((NZ, 2, NH, 2 * ROWS, HEAD), bf16),
            pltpu.VMEM((NY, NH, ROWS, HEAD), bf16),
            pltpu.VMEM((NY, NH, ROWS, HEAD), bf16),
            pltpu.VMEM((NY, NH, ROWS, HEAD), bf16),
            pltpu.VMEM((NY, NH, 8, ROWS), f32),
            pltpu.VMEM((NY, NH, 8, ROWS), f32),
            pltpu.VMEM((NH, 2, 2 * ROWS, HEAD), f32),
            pltpu.VMEM((NH, 2, 2 * ROWS, 1), f32),
            pltpu.VMEM((NH, 2, 2 * ROWS, 1), f32),
            pltpu.VMEM((ROWS, NH * HEAD), bf16),
            pltpu.VMEM((4, ROWS, COLS), f32),
            pltpu.VMEM((4, 8, ROWS), f32),
            pltpu.VMEM((4, 8, ROWS), f32),
            pltpu.VMEM((2, NP, ROWS, PART), bf16),
            pltpu.VMEM((2, NP, ROWS, PART), bf16),
            pltpu.VMEM((NP, ROWS, PART), bf16),
            pltpu.VMEM((NP, ROWS, PART), bf16),
            pltpu.VMEM((NP, ROWS, PART), f32),
            pltpu.VMEM((ROWS, COLS), f32),
            dma((NG,)),
            dma((NG, 2, 4)),
            dma((NG, NZ + 1)),
            dma((NG, 4)),
            dma((NG, 4)),
            dma((NY,)),
            dma((NY,)),
        ]
        + [dma((NG, NY))] * 4
        + [dma((4,))] * 4
        + [dma((2, NP))] * 2
        + [dma((NP,))] * 2
        + [dma((10,))],
        compiler_params=pltpu.CompilerParams(
            collective_id=0, has_side_effects=True, vmem_limit_bytes=56 * 2**20
        ),
        name="attention_block",
    )(
        query, query_gain, stale_keys, stale_values, hidden, out_weight,
        row(out_bias), row(residual_gate), row(norm_shift), row(norm_scale),
    )
    return pl.pallas_call(
        deliver,
        out_shape=(out, out),
        in_specs=[hbm] * 2,
        out_specs=(hbm, hbm),
        scratch_shapes=[dma((4,))],
        name="deliver",
    )(*results)


def solution(mesh):
    return jax.shard_map(
        body,
        mesh=mesh,
        in_specs=(
            P("patch", None),
            P("patch", "tensor"),
            P("tensor"),
            P("patch", "tensor"),
            P("patch", "tensor"),
            P("tensor", None),
            P(),
            P(),
            P(),
            P(),
        ),
        out_specs=(P("patch", "tensor"), P("patch", "tensor")),
        check_vma=False,
    )
```

time: 482 us -> 94.6 us (0.20)
  waiting for transfers between devices: 403 us -> 0 us
  Pallas kernels: 0 us -> 93.9 us
  local copies, waits for them, and re-layouts: 26.1 us -> 0 us
  matrix products: 21.1 us -> 0 us
  between operations: 13.9 us -> 0.64 us
  other arithmetic: 9.64 us -> 0 us
  blocking collectives: 8.25 us -> 0 us
    all_gather x2 -> x0, waiting for transfers between devices: 334 us -> none  [the longest x1 185 us: body(): lax.all_gather(stale_keys, 'patch', axis=0, tiled=True)]
    pallas_call x0 -> x2, Pallas kernels: none -> 93.9 us  [the longest x1 72.9 us: body(): pl.pallas_call(kernel, out_shape=(out, out), in_specs=[hbm] * 10, out_spe...]
    psum x1 -> x0, waiting for transfers between devices: 67.9 us -> none  [body(): full_branch = lax.psum(partial_out, 'tensor')]
    dot_general x3 -> x0, matrix products: 21.1 us -> none  [the longest x1 12.4 us: body(): jnp.einsum('htj,jhc->htc', expo.astype(jnp.bfloat16), values_piece, prefe...]
    all_gather x1 -> x0, local copies, waits for them, and re-layouts: 14.6 us -> none  [body(): lax.all_gather(stale_values, 'patch', axis=0, tiled=True)]
    unnamed x14 -> x0, local copies, waits for them, and re-layouts: 9.78 us -> none
    psum x1 -> x0, blocking collectives: 8.25 us -> none  [body(): squares = lax.psum(jnp.sum(query_wide * query_wide, axis=1), 'tensor')]
    reduce_sum x3 -> x0, other arithmetic: 7.18 us -> none  [the longest x1 4.17 us: body(): totals = jnp.sum(expo, axis=2)]
  transfers between devices with their start and end apart: 3 -> 0, of which waited for: 3 -> 0; matrix products, arithmetic and copies ran while one was open for 3% -> 0% of each run, Pallas kernels for 0% -> 0%
where the time goes in v2:
time: 94.6 us; the launch traced here: 94.5 us
  Pallas kernels  93.9 us (99%)
    pallas_call x1, Pallas kernels, body(): pl.pallas_call(kernel, out_shape=(out, out), in_specs=[hbm] * 10, out_spe...  72.9 us
    pallas_call x1, Pallas kernels, body(): pl.pallas_call(deliver, out_shape=(out, out), in_specs=[hbm] * 2, out_spe...  21 us

profile of v2, /device:TPU:1, one launch (start us, length us, event | category | flops | bytes accessed | tf_op | source)
XLA Modules:
  0.0 94.5 jit_solution(6754134612897995923)
XLA Ops:
  0.6 72.9 %attention_block.1 = (bf16[128,1280]{1,0:T(8,128)(2,1)}, bf16[128,1280]{1,0:T(8,128)(2,1)}) custom-call(bf16[128,640]{1,0:T(8,128)(2,1)} %query_hbm.1, f32[640]{0:T(1024)} %gain_hbm.1, bf16[128,640]{1,0:T(8,128)(2,1)} %keys_hbm.1, bf16[128,640]{1,0:T(8,128)(2,1)} %values_hbm.1, bf16[128,5120]{1,0:T(8,128)(2,1)} %hidden_hbm.1, bf16[640,5120]{1,0:T(8,128)(2,1)} %weight_hbm.1, ...), custom_call_target="tpu_custom_call" | custom-call | tf_op jit(solution)/shard_map/attention_block/pallas_call | solution.py:414
  73.5 21.0 %deliver.1 = (bf16[128,1280]{1,0:T(8,128)(2,1)}, bf16[128,1280]{1,0:T(8,128)(2,1)}) custom-call(bf16[128,1280]{1,0:T(8,128)(2,1)} %get-tuple-element.4.first_in, bf16[128,1280]{1,0:T(8,128)(2,1)} %get-tuple-element.5.second_in), custom_call_target="tpu_custom_call" | custom-call | tf_op jit(solution)/shard_map/deliver/pallas_call | solution.py:469

commit v3 on v2

--- a/solution.py
+++ b/solution.py
@@ -13,7 +13,7 @@
 HD = 2560
 ROWS = 128
 NH = 5
-GROUPS = ((0, 2), (2, 2), (4, 1))
+GROUPS = ((0, 1), (1, 2), (3, 1), (4, 1))
 NG = len(GROUPS)
 NZ = 8
 NY = 4
@@ -160,8 +160,8 @@
         if s != 3:
             pair(g, min(s, 3)).start()
 
-    for g in range(NG):
-        swap(g)
+    swap(0)
+    swap(1)
 
     def sq_copy(r):
         return remote(sq.at[0], sq.at[4 - r], sq_send.at[r], sq_recv.at[4 - r], tensor_dev(r))
@@ -169,7 +169,9 @@
     for r in range(1, 4):
         sq_copy(r).start()
     event(0, 0)
+    swap(2)
     event(1, 0)
+    swap(3)
     for r in range(1, 4):
         sq_copy(4 - r).wait_recv()
     factor = lax.rsqrt((sq[0] + sq[1] + sq[2] + sq[3]) / HD + 1e-06) * SCALE
@@ -184,12 +186,14 @@
 
     for r in range(NY):
         send_query(r)
+    event(0, 1)
     event(2, 0)
-    event(0, 1)
     event(1, 1)
+    event(0, 2)
+    event(3, 0)
+    event(2, 1)
     for r in range(NY):
         landed(qbuf.at[r], q_recv.at[r])
-    event(0, 2)
 
     def send_mixed(g, r, wait=False):
         back = (NY - r) % NY
@@ -268,47 +272,50 @@
             num = sum(shares[r] * orecv[r, h].astype(jnp.float32) for r in range(NY))
             attended[:, h * HEAD : (h + 1) * HEAD] = (num / den).astype(jnp.bfloat16)
 
-    def project(g, columns):
-        first, count = GROUPS[g]
+    def project(first, count, columns):
         rows = slice(first * HEAD, (first + count) * HEAD)
         return jnp.dot(attended[:, rows], weight[rows, columns], preferred_element_type=jnp.float32)
 
-    def project_early(g):
+    def project_early():
         def step(b, carry):
-            part = project(g, pl.ds(pl.multiple_of(b * COLS, COLS), COLS))
-            acc[b] = part if g == 0 else acc[b] + part
+            acc[b] = project(0, NH - 1, pl.ds(pl.multiple_of(b * COLS, COLS), COLS))
             return carry
 
         lax.fori_loop(0, 4, step, 0)
 
-    event(2, 1)
+    near(0)
     event(1, 2)
-    near(0)
     event(0, 3)
-    event(1, 3)
+    near(1)
+    event(3, 1)
     event(2, 2)
     event(0, 4)
-    near(1)
+    event(1, 3)
+    near(2)
+    far(0)
+    event(3, 2)
     event(2, 3)
+    near(3)
     event(1, 4)
-    far(0)
-    near(2)
+    copies[4].wait()
+    combine(0)
+    event(3, 3)
     event(2, 4)
     far(1)
-    copies[4].wait()
-    combine(0)
+    event(3, 4)
     far(2)
-    project_early(0)
+    far(3)
     combine(1)
-    project_early(1)
     combine(2)
+    project_early()
+    combine(3)
 
     for copy in copies[5:]:
         copy.wait()
 
     def branch_part(b, part):
         cols = pl.ds(pl.multiple_of(b * COLS + part * PART, PART), PART)
-        return acc[b, :, part * PART : (part + 1) * PART] + project(NG - 1, cols)
+        return acc[b, :, part * PART : (part + 1) * PART] + project(NH - 1, 1, cols)
 
     def sib_copy(i, part):
         return remote(tosib.at[i, part], fromsib.at[i, part], sib_send.at[i, part], sib_recv.at[i, part], sibling)
@@ -389,17 +396,9 @@
         st_copy(r).wait_send()
 
 
-def deliver(first_in, second_in, first_out, second_out, sems):
-    half = ROWS // 2
-    copies = [
-        pltpu.make_async_copy(src.at[pl.ds(i * half, half)], dst.at[pl.ds(i * half, half)], sems.at[2 * k + i])
-        for k, (src, dst) in enumerate(((first_in, first_out), (second_in, second_out)))
-        for i in range(2)
-    ]
-    for copy in copies:
-        copy.start()
-    for copy in copies:
-        copy.wait()
+def deliver(first_in, second_in, first_out, second_out):
+    first_out[...] = first_in[...]
+    second_out[...] = second_in[...]
 
 
 def body(
@@ -469,9 +468,9 @@
     return pl.pallas_call(
         deliver,
         out_shape=(out, out),
-        in_specs=[hbm] * 2,
-        out_specs=(hbm, hbm),
-        scratch_shapes=[dma((4,))],
+        in_specs=[vmem] * 2,
+        out_specs=(vmem, vmem),
+        compiler_params=pltpu.CompilerParams(vmem_limit_bytes=56 * 2**20),
         name="deliver",
     )(*results)
 

time: 94.6 us -> 74.1 us (0.78)
  Pallas kernels: 93.9 us -> 73.3 us
    pallas_call x1, Pallas kernels: 21 us -> 1.93 us  [body(): pl.pallas_call(deliver, out_shape=(out, out), in_specs=[vmem] * 2, out_sp...]
    pallas_call x1, Pallas kernels: 72.9 us -> 71.4 us  [body(): pl.pallas_call(kernel, out_shape=(out, out), in_specs=[hbm] * 10, out_spe...]
where the time goes in v3:
time: 74.1 us; the launch traced here: 74 us
  Pallas kernels  73.3 us (99%)
    pallas_call x1, Pallas kernels, body(): pl.pallas_call(kernel, out_shape=(out, out), in_specs=[hbm] * 10, out_spe...  71.4 us
    pallas_call x1, Pallas kernels, body(): pl.pallas_call(deliver, out_shape=(out, out), in_specs=[vmem] * 2, out_sp...  1.93 us

profile of v3, /device:TPU:1, one launch (start us, length us, event | category | flops | bytes accessed | tf_op | source)
XLA Modules:
  0.0 74.0 jit_solution(11258790769893119510)
XLA Ops:
  0.6 71.4 %attention_block.1 = (bf16[128,1280]{1,0:T(8,128)(2,1)}, bf16[128,1280]{1,0:T(8,128)(2,1)}) custom-call(bf16[128,640]{1,0:T(8,128)(2,1)} %query_hbm.1, f32[640]{0:T(1024)} %gain_hbm.1, bf16[128,640]{1,0:T(8,128)(2,1)} %keys_hbm.1, bf16[128,640]{1,0:T(8,128)(2,1)} %values_hbm.1, bf16[128,5120]{1,0:T(8,128)(2,1)} %hidden_hbm.1, bf16[640,5120]{1,0:T(8,128)(2,1)} %weight_hbm.1, ...), custom_call_target="tpu_custom_call" | custom-call | tf_op jit(solution)/shard_map/attention_block/pallas_call | solution.py:413
  72.0 1.9 %deliver.1 = (bf16[128,1280]{1,0:T(8,128)(2,1)}, bf16[128,1280]{1,0:T(8,128)(2,1)}) custom-call(bf16[128,1280]{1,0:T(8,128)(2,1)} %get-tuple-element.4.first_in, bf16[128,1280]{1,0:T(8,128)(2,1)} %get-tuple-element.5.second_in), custom_call_target="tpu_custom_call" | custom-call | tf_op jit(solution)/shard_map/deliver/pallas_call | solution.py:468

commit v4 on v3

--- a/solution.py
+++ b/solution.py
@@ -111,10 +111,17 @@
             return
         pl.when(jnp.logical_not(straight))(act)
         if not wait:
-            pl.when(straight)(pltpu.make_async_copy(src, dst, recv).start)
-
-    def landed(ref, recv):
-        remote(ref, ref, swap_send.at[0], recv, z_dev(1)).wait_recv()
+
+            @pl.when(straight)
+            def _():
+                dst[...] = src[...]
+
+    def landed(ref, recv, r=1):
+        wait = remote(ref, ref, swap_send.at[0], recv, z_dev(1)).wait_recv
+        if r > 0:
+            wait()
+        else:
+            pl.when(jnp.logical_not(straight))(wait)
 
     def heads(g):
         return pl.ds(*GROUPS[g])
@@ -151,7 +158,7 @@
 
     def event(g, s):
         if s == 0:
-            landed(block(g, 0, True), block_sem(g, 0, True))
+            landed(block(g, 0, True), block_sem(g, 0, True), 0)
         for up in (True, False):
             if s > 0:
                 landed(block(g, s, up), block_sem(g, s, up))
@@ -160,8 +167,8 @@
         if s != 3:
             pair(g, min(s, 3)).start()
 
-    swap(0)
-    swap(1)
+    for g in range(min(2, NG)):
+        swap(g)
 
     def sq_copy(r):
         return remote(sq.at[0], sq.at[4 - r], sq_send.at[r], sq_recv.at[4 - r], tensor_dev(r))
@@ -186,14 +193,8 @@
 
     for r in range(NY):
         send_query(r)
-    event(0, 1)
     event(2, 0)
-    event(1, 1)
-    event(0, 2)
     event(3, 0)
-    event(2, 1)
-    for r in range(NY):
-        landed(qbuf.at[r], q_recv.at[r])
 
     def send_mixed(g, r, wait=False):
         back = (NY - r) % NY
@@ -230,19 +231,21 @@
             osend[2 * j + i, h] = mixed[part]
             ssend[2 * j + i, h] = numbers[:, part]
 
-    def near(g, between=None):
-        for m in range(3):
-            pair(g, m).wait_recv()
+    def near(g, start, stop):
+        if start == 0:
+            for m in range(3):
+                pair(g, m).wait_recv()
         first, count = GROUPS[g]
 
         def step(i, carry):
             attend_near(first + i % count, 1 - i // count)
             return carry
 
-        lax.fori_loop(0, 2 * count, step, 0)
-
-    def far(g):
-        pair(g, 3).wait_recv()
+        lax.fori_loop(start, stop, step, 0)
+
+    def far(g, start, stop):
+        if start == 0:
+            pair(g, 3).wait_recv()
         first, count = GROUPS[g]
 
         def step(i, carry):
@@ -256,21 +259,21 @@
 
             return carry
 
-        lax.fori_loop(0, 2 * count, step, 0)
+        lax.fori_loop(start, stop, step, 0)
 
     def combine(g):
         for r in range(NY):
-            landed(orecv.at[r, heads(g)], o_recv.at[g, r])
-            landed(srecv.at[r, heads(g)], s_recv.at[g, r])
+            landed(orecv.at[r, heads(g)], o_recv.at[g, r], r)
+            landed(srecv.at[r, heads(g)], s_recv.at[g, r], r)
         first, count = GROUPS[g]
         for h in range(first, first + count):
-            numbers = jnp.transpose(jnp.concatenate([srecv[r, h] for r in range(NY)], axis=0))
-            tops = [numbers[:, 8 * r : 8 * r + 1] for r in range(NY)]
+            tops = [srecv[r, h, 0:1, :] for r in range(NY)]
             top = functools.reduce(jnp.maximum, tops)
             shares = [jnp.exp2(t - top) for t in tops]
-            den = sum(shares[r] * numbers[:, 8 * r + 1 : 8 * r + 2] for r in range(NY))
-            num = sum(shares[r] * orecv[r, h].astype(jnp.float32) for r in range(NY))
-            attended[:, h * HEAD : (h + 1) * HEAD] = (num / den).astype(jnp.bfloat16)
+            den = sum(shares[r] * srecv[r, h, 1:2, :] for r in range(NY))
+            scales = jnp.transpose(jnp.concatenate([share / den for share in shares] * 2, axis=0))
+            num = sum(scales[:, r : r + 1] * orecv[r, h].astype(jnp.float32) for r in range(NY))
+            attended[:, h * HEAD : (h + 1) * HEAD] = num.astype(jnp.bfloat16)
 
     def project(first, count, columns):
         rows = slice(first * HEAD, (first + count) * HEAD)
@@ -278,33 +281,42 @@
 
     def project_early():
         def step(b, carry):
-            acc[b] = project(0, NH - 1, pl.ds(pl.multiple_of(b * COLS, COLS), COLS))
+            acc[b] = project(0, GROUPS[-1][0], pl.ds(pl.multiple_of(b * COLS, COLS), COLS))
             return carry
 
         lax.fori_loop(0, 4, step, 0)
 
-    near(0)
+    event(0, 1)
+    event(1, 1)
+    event(2, 1)
+    event(3, 1)
+    event(0, 2)
+    for r in range(NY):
+        landed(qbuf.at[r], q_recv.at[r], r)
+    near(0, 0, 2)
     event(1, 2)
+    event(2, 2)
+    near(1, 0, 1)
+    event(3, 2)
+    near(1, 1, 2)
     event(0, 3)
-    near(1)
-    event(3, 1)
-    event(2, 2)
+    near(1, 2, 4)
+    near(2, 0, 2)
+    event(1, 3)
+    near(3, 0, 2)
+    event(2, 3)
+    event(3, 3)
     event(0, 4)
-    event(1, 3)
-    near(2)
-    far(0)
-    event(3, 2)
-    event(2, 3)
-    near(3)
     event(1, 4)
+    far(0, 0, 1)
+    event(2, 4)
+    far(0, 1, 2)
+    event(3, 4)
+    far(1, 0, 4)
+    far(2, 0, 2)
+    far(3, 0, 2)
     copies[4].wait()
     combine(0)
-    event(3, 3)
-    event(2, 4)
-    far(1)
-    event(3, 4)
-    far(2)
-    far(3)
     combine(1)
     combine(2)
     project_early()
@@ -315,7 +327,7 @@
 
     def branch_part(b, part):
         cols = pl.ds(pl.multiple_of(b * COLS + part * PART, PART), PART)
-        return acc[b, :, part * PART : (part + 1) * PART] + project(NH - 1, 1, cols)
+        return acc[b, :, part * PART : (part + 1) * PART] + project(*GROUPS[-1], cols)
 
     def sib_copy(i, part):
         return remote(tosib.at[i, part], fromsib.at[i, part], sib_send.at[i, part], sib_recv.at[i, part], sibling)

time: 74.1 us -> 72.7 us (0.981)
  Pallas kernels: 73.3 us -> 72 us
    pallas_call x1, Pallas kernels: 71.4 us -> 70.1 us  [body(): pl.pallas_call(kernel, out_shape=(out, out), in_specs=[hbm] * 10, out_spe...]
where the time goes in v4:
time: 72.7 us; the launch traced here: 72.6 us
  Pallas kernels  72 us (99%)
    pallas_call x1, Pallas kernels, body(): pl.pallas_call(kernel, out_shape=(out, out), in_specs=[hbm] * 10, out_spe...  70.1 us
    pallas_call x1, Pallas kernels, body(): pl.pallas_call(deliver, out_shape=(out, out), in_specs=[vmem] * 2, out_sp...  1.93 us

profile of v4, /device:TPU:1, one launch (start us, length us, event | category | flops | bytes accessed | tf_op | source)
XLA Modules:
  0.0 72.6 jit_solution(4525730251318323222)
XLA Ops:
  0.6 70.1 %attention_block.1 = (bf16[128,1280]{1,0:T(8,128)(2,1)}, bf16[128,1280]{1,0:T(8,128)(2,1)}) custom-call(bf16[128,640]{1,0:T(8,128)(2,1)} %query_hbm.1, f32[640]{0:T(1024)} %gain_hbm.1, bf16[128,640]{1,0:T(8,128)(2,1)} %keys_hbm.1, bf16[128,640]{1,0:T(8,128)(2,1)} %values_hbm.1, bf16[128,5120]{1,0:T(8,128)(2,1)} %hidden_hbm.1, bf16[640,5120]{1,0:T(8,128)(2,1)} %weight_hbm.1, ...), custom_call_target="tpu_custom_call" | custom-call | tf_op jit(solution)/shard_map/attention_block/pallas_call | solution.py:425
  70.7 1.9 %deliver.1 = (bf16[128,1280]{1,0:T(8,128)(2,1)}, bf16[128,1280]{1,0:T(8,128)(2,1)}) custom-call(bf16[128,1280]{1,0:T(8,128)(2,1)} %get-tuple-element.4.first_in, bf16[128,1280]{1,0:T(8,128)(2,1)} %get-tuple-element.5.second_in), custom_call_target="tpu_custom_call" | custom-call | tf_op jit(solution)/shard_map/deliver/pallas_call | solution.py:480

commit v5 on v4

--- a/solution.py
+++ b/solution.py
@@ -39,8 +39,8 @@
 
 
 def kernel(
-    query_hbm, gain_hbm, keys_hbm, values_hbm, hidden_hbm, weight_hbm, bias_hbm, gate_hbm, shift_hbm, norm_scale_hbm,
-    residual, modulated,
+    query_hbm, gain_hbm, keys_hbm, values_hbm, hidden_hbm, weight_hbm, bias_hbm, gate_hbm,
+    summed_hbm, moments,
     query, gain, keys, values, weight, hidden, params,
     kvstage, qstage, kv, qbuf, osend, orecv, ssend, srecv, near_mix, near_top, near_total, attended, acc,
     sq, stats, tosib, fromsib, tox, fromx, mine, summed,
@@ -77,7 +77,7 @@
     my_cols = pl.ds(pl.multiple_of(tensor * COLS, COLS), COLS)
     early = [(keys_hbm, keys), (values_hbm, values), (query_hbm, query), (gain_hbm, gain)]
     late = [(weight_hbm, weight), (hidden_hbm.at[:, my_cols], hidden)]
-    late += [(ref.at[:, my_cols], params.at[i]) for i, ref in enumerate((bias_hbm, gate_hbm, shift_hbm, norm_scale_hbm))]
+    late += [(ref.at[:, my_cols], params.at[i]) for i, ref in enumerate((bias_hbm, gate_hbm))]
     copies = [pltpu.make_async_copy(src, dst, local.at[i]) for i, (src, dst) in enumerate(early + late)]
     for copy in copies:
         copy.start()
@@ -193,6 +193,7 @@
 
     for r in range(NY):
         send_query(r)
+    event(0, 1)
     event(2, 0)
     event(3, 0)
 
@@ -210,21 +211,26 @@
         v = kv[first : first + count, :, h, ROWS : 2 * ROWS, :].reshape(count * 2 * ROWS, HEAD)
         return jnp.dot(expo.astype(jnp.bfloat16), v, preferred_element_type=jnp.float32)
 
+    def lane_sums(x):
+        return functools.reduce(jnp.add, [x[:, lo : lo + HEAD] for lo in range(0, x.shape[1], HEAD)])
+
     def attend_near(h, j):
         scores = scores_of(h, j, 0, NEAR)
         top = jnp.max(scores, axis=1, keepdims=True)
         expo = jnp.exp2(scores - top)
-        near_top[h, j] = top
-        near_total[h, j] = jnp.sum(expo, axis=1, keepdims=True)
+        near_top[h, j] = jnp.broadcast_to(top, (2 * ROWS, HEAD))
+        near_total[h, j] = lane_sums(expo)
         near_mix[h, j] = mix(h, expo, 0, NEAR)
 
     def attend_far(h, j):
-        scores = scores_of(h, j, NEAR, NZ - NEAR)
-        top = jnp.maximum(near_top[h, j], jnp.max(scores, axis=1, keepdims=True))
-        expo = jnp.exp2(scores - top)
-        fade = jnp.exp2(near_top[h, j] - top)
-        total = near_total[h, j] * fade + jnp.sum(expo, axis=1, keepdims=True)
-        mixed = (near_mix[h, j] * fade + mix(h, expo, NEAR, NZ - NEAR)).astype(jnp.bfloat16)
+        count = NZ - NEAR
+        scores = scores_of(h, j, NEAR, count)
+        old = near_top[h, j]
+        top = jnp.maximum(old, jnp.broadcast_to(jnp.max(scores, axis=1, keepdims=True), (2 * ROWS, HEAD)))
+        expo = jnp.exp2(scores - jnp.concatenate([top] * (2 * count), axis=1))
+        fade = jnp.exp2(old - top)
+        total = jnp.sum(near_total[h, j] * fade + lane_sums(expo), axis=1, keepdims=True)
+        mixed = (near_mix[h, j] * fade + mix(h, expo, NEAR, count)).astype(jnp.bfloat16)
         numbers = columns_to_rows(top, total)
         for i in range(2):
             part = slice(i * ROWS, (i + 1) * ROWS)
@@ -286,30 +292,29 @@
 
         lax.fori_loop(0, 4, step, 0)
 
-    event(0, 1)
     event(1, 1)
     event(2, 1)
+    event(0, 2)
     event(3, 1)
-    event(0, 2)
     for r in range(NY):
         landed(qbuf.at[r], q_recv.at[r], r)
     near(0, 0, 2)
     event(1, 2)
     event(2, 2)
     near(1, 0, 1)
+    event(0, 3)
+    near(1, 1, 2)
     event(3, 2)
-    near(1, 1, 2)
-    event(0, 3)
     near(1, 2, 4)
     near(2, 0, 2)
+    event(2, 3)
     event(1, 3)
+    event(0, 4)
     near(3, 0, 2)
-    event(2, 3)
     event(3, 3)
-    event(0, 4)
+    event(2, 4)
+    far(0, 0, 1)
     event(1, 4)
-    far(0, 0, 1)
-    event(2, 4)
     far(0, 1, 2)
     event(3, 4)
     far(1, 0, 4)
@@ -362,11 +367,12 @@
         x_copy(part).wait_recv()
         value = mine[part] + params[1, :, cols] * fromx[part].astype(jnp.float32)
         summed[:, cols] = value
-        residual[:, cols] = value.astype(jnp.bfloat16)
         for lo in range(0, PART, HEAD):
             piece = value[:, lo : lo + HEAD]
             total = total + piece
             total_sq = total_sq + piece * piece
+    keep = pltpu.make_async_copy(summed, summed_hbm, local.at[0])
+    keep.start()
     stats[0] = columns_to_rows(
         jnp.sum(total, axis=1, keepdims=True), jnp.sum(total_sq, axis=1, keepdims=True)
     )
@@ -397,20 +403,21 @@
 
     for r in range(1, 4):
         st_copy(4 - r).wait_recv()
-    both = jnp.transpose(stats[0] + stats[1] + stats[2] + stats[3]) / D
-    mean = both[:, 0:1]
-    inv = lax.rsqrt(both[:, 1:2] - mean * mean + 1e-06)
-    for part in range(NP):
-        cols = slice(part * PART, (part + 1) * PART)
-        value = (summed[:, cols] - mean) * inv * (1.0 + params[3, :, cols]) + params[2, :, cols]
-        modulated[:, cols] = value.astype(jnp.bfloat16)
+    sums = (stats[0] + stats[1] + stats[2] + stats[3]) / D
+    mean = sums[0:1, :]
+    moments[...] = jnp.concatenate([mean, lax.rsqrt(sums[1:8, :] - mean * mean + 1e-06)], axis=0)
+    keep.wait()
     for r in range(1, 4):
         st_copy(r).wait_send()
 
 
-def deliver(first_in, second_in, first_out, second_out):
-    first_out[...] = first_in[...]
-    second_out[...] = second_in[...]
+def normalise(summed, moments, shift, scale, residual, modulated):
+    columns = jnp.transpose(moments[...])
+    mean, inv = columns[:, 0:1], columns[:, 1:2]
+    my_cols = pl.ds(pl.multiple_of(lax.axis_index("tensor") * COLS, COLS), COLS)
+    value = summed[...]
+    residual[...] = value.astype(jnp.bfloat16)
+    modulated[...] = ((value - mean) * inv * (1.0 + scale[:, my_cols]) + shift[:, my_cols]).astype(jnp.bfloat16)
 
 
 def body(
@@ -422,11 +429,11 @@
     dma = pltpu.SemaphoreType.DMA
     row = lambda x: x.reshape(1, -1)
     out = jax.ShapeDtypeStruct((ROWS, COLS), bf16)
-    results = pl.pallas_call(
+    summed, moments = pl.pallas_call(
         kernel,
-        out_shape=(out, out),
-        in_specs=[hbm] * 10,
-        out_specs=(vmem, vmem),
+        out_shape=(jax.ShapeDtypeStruct((ROWS, COLS), f32), jax.ShapeDtypeStruct((8, ROWS), f32)),
+        in_specs=[hbm] * 8,
+        out_specs=(hbm, vmem),
         scratch_shapes=[
             pltpu.VMEM((ROWS, NH * HEAD), bf16),
             pltpu.VMEM((NH * HEAD,), f32),
@@ -434,7 +441,7 @@
             pltpu.VMEM((ROWS, NH * HEAD), bf16),
             pltpu.VMEM((NH * HEAD, D), bf16),
             pltpu.VMEM((ROWS, COLS), bf16),
-            pltpu.VMEM((4, 1, COLS), f32),
+            pltpu.VMEM((2, 1, COLS), f32),
             pltpu.VMEM((NH, 2 * ROWS, HEAD), bf16),
             pltpu.VMEM((NH, ROWS, HEAD), bf16),
             pltpu.VMEM((NZ, 2, NH, 2 * ROWS, HEAD), bf16),
@@ -444,8 +451,8 @@
             pltpu.VMEM((NY, NH, 8, ROWS), f32),
             pltpu.VMEM((NY, NH, 8, ROWS), f32),
             pltpu.VMEM((NH, 2, 2 * ROWS, HEAD), f32),
-            pltpu.VMEM((NH, 2, 2 * ROWS, 1), f32),
-            pltpu.VMEM((NH, 2, 2 * ROWS, 1), f32),
+            pltpu.VMEM((NH, 2, 2 * ROWS, HEAD), f32),
+            pltpu.VMEM((NH, 2, 2 * ROWS, HEAD), f32),
             pltpu.VMEM((ROWS, NH * HEAD), bf16),
             pltpu.VMEM((4, ROWS, COLS), f32),
             pltpu.VMEM((4, 8, ROWS), f32),
@@ -468,23 +475,23 @@
         + [dma((4,))] * 4
         + [dma((2, NP))] * 2
         + [dma((NP,))] * 2
-        + [dma((10,))],
+        + [dma((8,))],
         compiler_params=pltpu.CompilerParams(
             collective_id=0, has_side_effects=True, vmem_limit_bytes=56 * 2**20
         ),
         name="attention_block",
     )(
         query, query_gain, stale_keys, stale_values, hidden, out_weight,
-        row(out_bias), row(residual_gate), row(norm_shift), row(norm_scale),
+        row(out_bias), row(residual_gate),
     )
     return pl.pallas_call(
-        deliver,
+        normalise,
         out_shape=(out, out),
-        in_specs=[vmem] * 2,
+        in_specs=[vmem] * 4,
         out_specs=(vmem, vmem),
         compiler_params=pltpu.CompilerParams(vmem_limit_bytes=56 * 2**20),
-        name="deliver",
-    )(*results)
+        name="normalise",
+    )(summed, moments, row(norm_shift), row(norm_scale))
 
 
 def solution(mesh):

time: 72.7 us -> 70.9 us (0.975)
  Pallas kernels: 72 us -> 70.2 us
    pallas_call x2, Pallas kernels: 72 us -> 70.2 us  [the longest x1 68 us: body(): pl.pallas_call(kernel, out_shape=(jax.ShapeDtypeStruct((ROWS, COLS), f32)...]
where the time goes in v5:
time: 70.9 us; the launch traced here: 70.8 us
  Pallas kernels  70.2 us (99%)
    pallas_call x1, Pallas kernels, body(): pl.pallas_call(kernel, out_shape=(jax.ShapeDtypeStruct((ROWS, COLS), f32)...  68 us
    pallas_call x1, Pallas kernels, body(): pl.pallas_call(normalise, out_shape=(out, out), in_specs=[vmem] * 4, out_...  2.16 us

profile of v5, /device:TPU:1, one launch (start us, length us, event | category | flops | bytes accessed | tf_op | source)
XLA Modules:
  0.0 70.8 jit_solution(16318003746554965122)
XLA Ops:
  0.6 68.0 %attention_block.1 = (f32[128,1280]{1,0:T(8,128)}, f32[8,128]{1,0:T(8,128)}) custom-call(bf16[128,640]{1,0:T(8,128)(2,1)} %query_hbm.1, f32[640]{0:T(1024)} %gain_hbm.1, bf16[128,640]{1,0:T(8,128)(2,1)} %keys_hbm.1, bf16[128,640]{1,0:T(8,128)(2,1)} %values_hbm.1, bf16[128,5120]{1,0:T(8,128)(2,1)} %hidden_hbm.1, bf16[640,5120]{1,0:T(8,128)(2,1)} %weight_hbm.1, ...), custom_call_target="tpu_custom_call" | custom-call | tf_op jit(solution)/shard_map/attention_block/pallas_call | solution.py:432
  68.7 2.2 %normalise.1 = (bf16[128,1280]{1,0:T(8,128)(2,1)}, bf16[128,1280]{1,0:T(8,128)(2,1)}) custom-call(f32[128,1280]{1,0:T(8,128)} %get-tuple-element.4.summed, f32[8,128]{1,0:T(8,128)} %get-tuple-element.5.moments, f32[1,5120]{1,0:T(1,128)} %bitcast.6, f32[1,5120]{1,0:T(1,128)} %bitcast.7), custom_call_target="tpu_custom_call" | custom-call | tf_op jit(solution)/shard_map/normalise/pallas_call | solution.py:487

commit v6 on v5

--- a/solution.py
+++ b/solution.py
@@ -18,6 +18,8 @@
 NZ = 8
 NY = 4
 NEAR = 5
+HALF = ROWS // 2
+BOTH = 2
 COLS = 1280
 PART = 256
 NP = COLS // PART
@@ -42,10 +44,10 @@
     query_hbm, gain_hbm, keys_hbm, values_hbm, hidden_hbm, weight_hbm, bias_hbm, gate_hbm,
     summed_hbm, moments,
     query, gain, keys, values, weight, hidden, params,
-    kvstage, qstage, kv, qbuf, osend, orecv, ssend, srecv, near_mix, near_top, near_total, attended, acc,
+    kvstage, qstage, kv, qbuf, osend, orecv, ssend, srecv, near_mix, near_top, near_total, attended, crossing, otwin, stwin, acc,
     sq, stats, tosib, fromsib, tox, fromx, mine, summed,
     swap_send, kv_send, kv_recv, pair_send, pair_recv, q_send, q_recv, o_send, o_recv, s_send, s_recv, sq_send, sq_recv,
-    st_send, st_recv, sib_send, sib_recv, x_send, x_recv, local,
+    st_send, st_recv, sib_send, sib_recv, x_send, x_recv, ot_send, ot_recv, stt_send, stt_recv, half_send, half_recv, local,
 ):
     patch = lax.axis_index("patch")
     tensor = lax.axis_index("tensor")
@@ -65,8 +67,21 @@
     sibling = {"patch": patch, "tensor": xl * 2 + (1 - core)}
     across = {"patch": patch, "tensor": (1 - xl) * 2 + core}
 
+    def twin_like(r):
+        return {"patch": ((y + r) % NY) * 16 + z * 2 + (1 - xh), "tensor": tensor}
+
+    def sibling_like(r):
+        return {"patch": ((y + r) % NY) * 16 + z * 2 + xh, "tensor": xl * 2 + (1 - core)}
+
+    def group_twin(r):
+        return {"patch": ((y + r) % NY) * 16 + z * 2 + (1 - core), "tensor": xl * 2 + xh}
+
+    twin = twin_like(0)
+    across_twin = {"patch": y * 16 + z * 2 + (1 - xh), "tensor": (1 - xl) * 2 + core}
+
     barrier = pltpu.get_barrier_semaphore()
     partners = [z_dev(1), z_dev(-1)] + [group_dev(r) for r in range(1, NY)] + [tensor_dev(r) for r in range(1, 4)]
+    partners += [twin_like(r) for r in range(NY)] + [sibling_like(r) for r in range(1, NY)] + [across_twin]
     for device in partners:
         pl.semaphore_signal(barrier, inc=1, device_id=device, device_id_type=MESH)
 
@@ -201,6 +216,13 @@
         back = (NY - r) % NY
         to_group(osend.at[r, heads(g)], orecv.at[back, heads(g)], o_send.at[g, r], o_recv.at[g, back], r, wait)
         to_group(ssend.at[r, heads(g)], srecv.at[back, heads(g)], s_send.at[g, r], s_recv.at[g, back], r, wait)
+
+    def to_twin(g, r):
+        (h, _), i, back = GROUPS[g], g - BOTH, (NY - r) % NY
+        return (
+            remote(osend.at[r, h, pl.ds(HALF, HALF)], otwin.at[i, back], ot_send.at[i, r], ot_recv.at[i, back], group_twin(r)),
+            remote(ssend.at[r, h], stwin.at[i, back], stt_send.at[i, r], stt_recv.at[i, back], group_twin(r)),
+        )
 
     def scores_of(h, j, first, count):
         q = qbuf[pl.ds(2 * j, 2), h].reshape(2 * ROWS, HEAD)
@@ -260,12 +282,22 @@
 
                 @pl.when(i == (2 - j) * count - 1)
                 def _(j=j):
-                    send_mixed(g, 2 * j + 1)
-                    send_mixed(g, 2 * j)
+                    for r in (2 * j + 1, 2 * j):
+                        send_mixed(g, r)
+                        if g >= BOTH:
+                            for copy in to_twin(g, r):
+                                copy.start()
 
             return carry
 
         lax.fori_loop(start, stop, step, 0)
+
+    def merge_scales(numbers):
+        tops = [x[0:1, :] for x in numbers]
+        top = functools.reduce(jnp.maximum, tops)
+        shares = [jnp.exp2(t - top) for t in tops]
+        den = sum(share * x[1:2, :] for share, x in zip(shares, numbers))
+        return jnp.transpose(jnp.concatenate([share / den for share in shares] * 2, axis=0))
 
     def combine(g):
         for r in range(NY):
@@ -273,24 +305,39 @@
             landed(srecv.at[r, heads(g)], s_recv.at[g, r], r)
         first, count = GROUPS[g]
         for h in range(first, first + count):
-            tops = [srecv[r, h, 0:1, :] for r in range(NY)]
-            top = functools.reduce(jnp.maximum, tops)
-            shares = [jnp.exp2(t - top) for t in tops]
-            den = sum(shares[r] * srecv[r, h, 1:2, :] for r in range(NY))
-            scales = jnp.transpose(jnp.concatenate([share / den for share in shares] * 2, axis=0))
+            scales = merge_scales([srecv[r, h] for r in range(NY)])
             num = sum(scales[:, r : r + 1] * orecv[r, h].astype(jnp.float32) for r in range(NY))
             attended[:, h * HEAD : (h + 1) * HEAD] = num.astype(jnp.bfloat16)
 
-    def project(first, count, columns):
+    def combine_twin(g):
+        (h, _), i = GROUPS[g], g - BOTH
+        for r in range(NY):
+            landed(otwin.at[i, r], ot_recv.at[i, r])
+            landed(stwin.at[i, r], stt_recv.at[i, r])
+        scales = merge_scales([stwin[i, r] for r in range(NY)])[HALF:]
+        num = sum(scales[:, r : r + 1] * otwin[i, r].astype(jnp.float32) for r in range(NY))
+        crossing[HALF:, h * HEAD : (h + 1) * HEAD] = num.astype(jnp.bfloat16)
+        crossing[0:HALF, h * HEAD : (h + 1) * HEAD] = attended[0:HALF, h * HEAD : (h + 1) * HEAD]
+
+    first_lanes = pl.ds(0, GROUPS[BOTH][0] * HEAD)
+
+    def half_copy():
+        return remote(
+            attended.at[pl.ds(HALF, HALF), first_lanes], crossing.at[pl.ds(HALF, HALF), first_lanes],
+            half_send.at[0], half_recv.at[0], twin,
+        )
+
+    def project(source, first, count, columns):
         rows = slice(first * HEAD, (first + count) * HEAD)
-        return jnp.dot(attended[:, rows], weight[rows, columns], preferred_element_type=jnp.float32)
-
-    def project_early():
-        def step(b, carry):
-            acc[b] = project(0, GROUPS[-1][0], pl.ds(pl.multiple_of(b * COLS, COLS), COLS))
+        return jnp.dot(source[:, rows], weight[rows, columns], preferred_element_type=jnp.float32)
+
+    def project_early(source, chip):
+        def step(i, carry):
+            b = chip * 2 + i
+            acc[b] = project(source, 0, NH - 1, pl.ds(pl.multiple_of(b * COLS, COLS), COLS))
             return carry
 
-        lax.fori_loop(0, 4, step, 0)
+        lax.fori_loop(0, 2, step, 0)
 
     event(1, 1)
     event(2, 1)
@@ -323,38 +370,49 @@
     copies[4].wait()
     combine(0)
     combine(1)
+    half_copy().start()
+    crossing[0:HALF, 0 : GROUPS[BOTH][0] * HEAD] = attended[0:HALF, 0 : GROUPS[BOTH][0] * HEAD]
     combine(2)
-    project_early()
+    combine_twin(2)
+    project_early(attended, xl)
+    half_copy().wait_recv()
+    project_early(crossing, 1 - xl)
     combine(3)
+    combine_twin(3)
 
     for copy in copies[5:]:
         copy.wait()
 
-    def branch_part(b, part):
+    def branch_part(source, b, part):
         cols = pl.ds(pl.multiple_of(b * COLS + part * PART, PART), PART)
-        return acc[b, :, part * PART : (part + 1) * PART] + project(*GROUPS[-1], cols)
+        return acc[b, :, part * PART : (part + 1) * PART] + project(source, NH - 1, 1, cols)
 
     def sib_copy(i, part):
         return remote(tosib.at[i, part], fromsib.at[i, part], sib_send.at[i, part], sib_recv.at[i, part], sibling)
 
-    def x_copy(part):
-        return remote(tox.at[part], fromx.at[part], x_send.at[part], x_recv.at[part], across)
-
-    def stage(i, b):
+    def x_copies(part):
+        halves = pl.ds(0, HALF), pl.ds(HALF, HALF)
+        return [
+            remote(tox.at[part, half], fromx.at[part, half], x_send.at[i, part], x_recv.at[i, part], device)
+            for i, (half, device) in enumerate(zip(halves, (across, across_twin)))
+        ]
+
+    def stage(i, source, b):
         for part in range(NP):
-            tosib[i, part] = branch_part(b, part).astype(jnp.bfloat16)
+            tosib[i, part] = branch_part(source, b, part).astype(jnp.bfloat16)
             sib_copy(i, part).start()
 
-    stage(0, (1 - xl) * 2 + (1 - core))
+    stage(0, crossing, (1 - xl) * 2 + (1 - core))
     for part in range(NP):
-        ours = branch_part((1 - xl) * 2 + core, part)
+        ours = branch_part(crossing, (1 - xl) * 2 + core, part)
         sib_copy(0, part).wait_recv()
         tox[part] = (ours + fromsib[0, part].astype(jnp.float32)).astype(jnp.bfloat16)
-        x_copy(part).start()
-    stage(1, xl * 2 + (1 - core))
+        for copy in x_copies(part):
+            copy.start()
+    stage(1, attended, xl * 2 + (1 - core))
     for part in range(NP):
         cols = slice(part * PART, (part + 1) * PART)
-        branch = branch_part(tensor, part) + params[0, :, cols]
+        branch = branch_part(attended, tensor, part) + params[0, :, cols]
         sib_copy(1, part).wait_recv()
         mine[part] = hidden[:, cols].astype(jnp.float32) + params[1, :, cols] * (
             branch + fromsib[1, part].astype(jnp.float32)
@@ -364,7 +422,8 @@
     total_sq = jnp.zeros((ROWS, HEAD), jnp.float32)
     for part in range(NP):
         cols = slice(part * PART, (part + 1) * PART)
-        x_copy(part).wait_recv()
+        for copy in x_copies(part):
+            copy.wait_recv()
         value = mine[part] + params[1, :, cols] * fromx[part].astype(jnp.float32)
         summed[:, cols] = value
         for lo in range(0, PART, HEAD):
@@ -392,14 +451,19 @@
             pair(g, m).wait_send()
         for r in range(NY):
             send_mixed(g, r, wait=True)
+            if g >= BOTH:
+                for copy in to_twin(g, r):
+                    copy.wait_send()
     for r in range(NY):
         send_query(r, wait=True)
+    half_copy().wait_send()
     for r in range(1, 4):
         sq_copy(r).wait_send()
     for part in range(NP):
         sib_copy(0, part).wait_send()
         sib_copy(1, part).wait_send()
-        x_copy(part).wait_send()
+        for copy in x_copies(part):
+            copy.wait_send()
 
     for r in range(1, 4):
         st_copy(4 - r).wait_recv()
@@ -454,6 +518,9 @@
             pltpu.VMEM((NH, 2, 2 * ROWS, HEAD), f32),
             pltpu.VMEM((NH, 2, 2 * ROWS, HEAD), f32),
             pltpu.VMEM((ROWS, NH * HEAD), bf16),
+            pltpu.VMEM((ROWS, NH * HEAD), bf16),
+            pltpu.VMEM((NG - BOTH, NY, HALF, HEAD), bf16),
+            pltpu.VMEM((NG - BOTH, NY, 8, ROWS), f32),
             pltpu.VMEM((4, ROWS, COLS), f32),
             pltpu.VMEM((4, 8, ROWS), f32),
             pltpu.VMEM((4, 8, ROWS), f32),
@@ -474,7 +541,9 @@
         + [dma((NG, NY))] * 4
         + [dma((4,))] * 4
         + [dma((2, NP))] * 2
-        + [dma((NP,))] * 2
+        + [dma((2, NP))] * 2
+        + [dma((NG - BOTH, NY))] * 4
+        + [dma((1,))] * 2
         + [dma((8,))],
         compiler_params=pltpu.CompilerParams(
             collective_id=0, has_side_effects=True, vmem_limit_bytes=56 * 2**20

time: 70.9 us -> 71.6 us (level)
  no operation moved by 1% of the time
where the time goes in v6:
time: 71.6 us; the launch traced here: 71.5 us
  Pallas kernels  70.9 us (99%)
    pallas_call x1, Pallas kernels, body(): pl.pallas_call(kernel, out_shape=(jax.ShapeDtypeStruct((ROWS, COLS), f32)...  68.7 us
    pallas_call x1, Pallas kernels, body(): pl.pallas_call(normalise, out_shape=(out, out), in_specs=[vmem] * 4, out_...  2.16 us

profile of v6, /device:TPU:1, one launch (start us, length us, event | category | flops | bytes accessed | tf_op | source)
XLA Modules:
  0.0 71.5 jit_solution(10054146952478285660)
XLA Ops:
  0.6 68.7 %attention_block.1 = (f32[128,1280]{1,0:T(8,128)}, f32[8,128]{1,0:T(8,128)}) custom-call(bf16[128,640]{1,0:T(8,128)(2,1)} %query_hbm.1, f32[640]{0:T(1024)} %gain_hbm.1, bf16[128,640]{1,0:T(8,128)(2,1)} %keys_hbm.1, bf16[128,640]{1,0:T(8,128)(2,1)} %values_hbm.1, bf16[128,5120]{1,0:T(8,128)(2,1)} %hidden_hbm.1, bf16[640,5120]{1,0:T(8,128)(2,1)} %weight_hbm.1, ...), custom_call_target="tpu_custom_call" | custom-call | tf_op jit(solution)/shard_map/attention_block/pallas_call | solution.py:496
  69.4 2.2 %normalise.1 = (bf16[128,1280]{1,0:T(8,128)(2,1)}, bf16[128,1280]{1,0:T(8,128)(2,1)}) custom-call(f32[128,1280]{1,0:T(8,128)} %get-tuple-element.4.summed, f32[8,128]{1,0:T(8,128)} %get-tuple-element.5.moments, f32[1,5120]{1,0:T(1,128)} %bitcast.6, f32[1,5120]{1,0:T(1,128)} %bitcast.7), custom_call_target="tpu_custom_call" | custom-call | tf_op jit(solution)/shard_map/normalise/pallas_call | solution.py:556

commit v7 on v5

--- a/solution.py
+++ b/solution.py
@@ -13,11 +13,11 @@
 HD = 2560
 ROWS = 128
 NH = 5
-GROUPS = ((0, 1), (1, 2), (3, 1), (4, 1))
+GROUPS = ((0, 1), (1, 1), (2, 2), (4, 1))
 NG = len(GROUPS)
 NZ = 8
 NY = 4
-NEAR = 5
+PARTS = ((0, 3), (3, 2), (5, 2), (7, 1))
 COLS = 1280
 PART = 256
 NP = COLS // PART
@@ -42,7 +42,7 @@
     query_hbm, gain_hbm, keys_hbm, values_hbm, hidden_hbm, weight_hbm, bias_hbm, gate_hbm,
     summed_hbm, moments,
     query, gain, keys, values, weight, hidden, params,
-    kvstage, qstage, kv, qbuf, osend, orecv, ssend, srecv, near_mix, near_top, near_total, attended, acc,
+    kvstage, qstage, kv, qbuf, osend, orecv, ssend, srecv, run_mix, run_top, run_total, attended, acc,
     sq, stats, tosib, fromsib, tox, fromx, mine, summed,
     swap_send, kv_send, kv_recv, pair_send, pair_recv, q_send, q_recv, o_send, o_recv, s_send, s_recv, sq_send, sq_recv,
     st_send, st_recv, sib_send, sib_recv, x_send, x_recv, local,
@@ -148,7 +148,7 @@
             src, block(g, s + 1, up), kv_send.at[g, int(up), s], block_sem(g, s + 1, up), z_dev(1 if up else -1)
         )
 
-    shares = ((0, 1), (1, 2), (3, 2), (5, 3))
+    shares = ((0, 1), (1, 2), (3, 2), (5, 2), (7, 1))
 
     def pair(g, m):
         places = pl.ds(*shares[m])
@@ -164,8 +164,7 @@
                 landed(block(g, s, up), block_sem(g, s, up))
             if s < 4:
                 hop(g, s, up).start()
-        if s != 3:
-            pair(g, min(s, 3)).start()
+        pair(g, s).start()
 
     for g in range(min(2, NG)):
         swap(g)
@@ -193,79 +192,72 @@
 
     for r in range(NY):
         send_query(r)
-    event(0, 1)
     event(2, 0)
     event(3, 0)
+    event(0, 1)
+    event(1, 1)
+    event(2, 1)
 
     def send_mixed(g, r, wait=False):
         back = (NY - r) % NY
         to_group(osend.at[r, heads(g)], orecv.at[back, heads(g)], o_send.at[g, r], o_recv.at[g, back], r, wait)
         to_group(ssend.at[r, heads(g)], srecv.at[back, heads(g)], s_send.at[g, r], s_recv.at[g, back], r, wait)
 
-    def scores_of(h, j, first, count):
-        q = qbuf[pl.ds(2 * j, 2), h].reshape(2 * ROWS, HEAD)
-        k = kv[first : first + count, :, h, 0:ROWS, :].reshape(count * 2 * ROWS, HEAD)
-        return lax.dot_general(q, k, CONTRACT_LAST, preferred_element_type=jnp.float32)
-
-    def mix(h, expo, first, count):
-        v = kv[first : first + count, :, h, ROWS : 2 * ROWS, :].reshape(count * 2 * ROWS, HEAD)
-        return jnp.dot(expo.astype(jnp.bfloat16), v, preferred_element_type=jnp.float32)
-
     def lane_sums(x):
         return functools.reduce(jnp.add, [x[:, lo : lo + HEAD] for lo in range(0, x.shape[1], HEAD)])
 
-    def attend_near(h, j):
-        scores = scores_of(h, j, 0, NEAR)
-        top = jnp.max(scores, axis=1, keepdims=True)
-        expo = jnp.exp2(scores - top)
-        near_top[h, j] = jnp.broadcast_to(top, (2 * ROWS, HEAD))
-        near_total[h, j] = lane_sums(expo)
-        near_mix[h, j] = mix(h, expo, 0, NEAR)
-
-    def attend_far(h, j):
-        count = NZ - NEAR
-        scores = scores_of(h, j, NEAR, count)
-        old = near_top[h, j]
-        top = jnp.maximum(old, jnp.broadcast_to(jnp.max(scores, axis=1, keepdims=True), (2 * ROWS, HEAD)))
+    def attend(h, part):
+        first, count = PARTS[part]
+        q = qbuf[:, h].reshape(NY * ROWS, HEAD)
+        k = kv[first : first + count, :, h, 0:ROWS, :].reshape(count * 2 * ROWS, HEAD)
+        v = kv[first : first + count, :, h, ROWS : 2 * ROWS, :].reshape(count * 2 * ROWS, HEAD)
+        scores = lax.dot_general(q, k, CONTRACT_LAST, preferred_element_type=jnp.float32)
+        top = jnp.broadcast_to(jnp.max(scores, axis=1, keepdims=True), (NY * ROWS, HEAD))
+        if part > 0:
+            old = run_top[h]
+            top = jnp.maximum(old, top)
+            fade = jnp.exp2(old - top)
         expo = jnp.exp2(scores - jnp.concatenate([top] * (2 * count), axis=1))
-        fade = jnp.exp2(old - top)
-        total = jnp.sum(near_total[h, j] * fade + lane_sums(expo), axis=1, keepdims=True)
-        mixed = (near_mix[h, j] * fade + mix(h, expo, NEAR, count)).astype(jnp.bfloat16)
-        numbers = columns_to_rows(top, total)
-        for i in range(2):
-            part = slice(i * ROWS, (i + 1) * ROWS)
-            osend[2 * j + i, h] = mixed[part]
-            ssend[2 * j + i, h] = numbers[:, part]
-
-    def near(g, start, stop):
-        if start == 0:
-            for m in range(3):
-                pair(g, m).wait_recv()
-        first, count = GROUPS[g]
-
-        def step(i, carry):
-            attend_near(first + i % count, 1 - i // count)
+        total = lane_sums(expo)
+        mixed = jnp.dot(expo.astype(jnp.bfloat16), v, preferred_element_type=jnp.float32)
+        if part > 0:
+            total = run_total[h] * fade + total
+            mixed = run_mix[h] * fade + mixed
+        if part < len(PARTS) - 1:
+            run_top[h] = top
+            run_total[h] = total
+            run_mix[h] = mixed
+            return
+        numbers = columns_to_rows(top, jnp.sum(total, axis=1, keepdims=True))
+        for r in range(NY):
+            rows = slice(r * ROWS, (r + 1) * ROWS)
+            osend[r, h] = mixed[rows].astype(jnp.bfloat16)
+            ssend[r, h] = numbers[:, rows]
+
+    def sweep(part, events):
+        def step(h, carry):
+            for g, (first, count) in enumerate(GROUPS):
+
+                @pl.when(h == first)
+                def _(g=g):
+                    for due in events.get(g, ()):
+                        event(*due)
+                    if part == 0:
+                        pair(g, 0).wait_recv()
+                    pair(g, part + 1).wait_recv()
+
+            attend(h, part)
+            if part == len(PARTS) - 1:
+                for g, (first, count) in enumerate(GROUPS):
+
+                    @pl.when(h == first + count - 1)
+                    def _(g=g):
+                        for r in (2, 1, 3, 0):
+                            send_mixed(g, r)
+
             return carry
 
-        lax.fori_loop(start, stop, step, 0)
-
-    def far(g, start, stop):
-        if start == 0:
-            pair(g, 3).wait_recv()
-        first, count = GROUPS[g]
-
-        def step(i, carry):
-            attend_far(first + i % count, 1 - i // count)
-            for j in (1, 0):
-
-                @pl.when(i == (2 - j) * count - 1)
-                def _(j=j):
-                    send_mixed(g, 2 * j + 1)
-                    send_mixed(g, 2 * j)
-
-            return carry
-
-        lax.fori_loop(start, stop, step, 0)
+        lax.fori_loop(0, NH, step, 0)
 
     def combine(g):
         for r in range(NY):
@@ -292,34 +284,14 @@
 
         lax.fori_loop(0, 4, step, 0)
 
-    event(1, 1)
-    event(2, 1)
-    event(0, 2)
-    event(3, 1)
     for r in range(NY):
         landed(qbuf.at[r], q_recv.at[r], r)
-    near(0, 0, 2)
+    sweep(0, {2: [(3, 1)], 3: [(0, 2)]})
     event(1, 2)
-    event(2, 2)
-    near(1, 0, 1)
-    event(0, 3)
-    near(1, 1, 2)
-    event(3, 2)
-    near(1, 2, 4)
-    near(2, 0, 2)
-    event(2, 3)
+    sweep(1, {2: [(2, 2), (3, 2)], 3: [(0, 3)]})
     event(1, 3)
-    event(0, 4)
-    near(3, 0, 2)
-    event(3, 3)
-    event(2, 4)
-    far(0, 0, 1)
-    event(1, 4)
-    far(0, 1, 2)
-    event(3, 4)
-    far(1, 0, 4)
-    far(2, 0, 2)
-    far(3, 0, 2)
+    sweep(2, {2: [(2, 3), (3, 3), (0, 4)], 3: [(1, 4)]})
+    sweep(3, {1: [(2, 4), (3, 4)]})
     copies[4].wait()
     combine(0)
     combine(1)
@@ -450,9 +422,9 @@
             pltpu.VMEM((NY, NH, ROWS, HEAD), bf16),
             pltpu.VMEM((NY, NH, 8, ROWS), f32),
             pltpu.VMEM((NY, NH, 8, ROWS), f32),
-            pltpu.VMEM((NH, 2, 2 * ROWS, HEAD), f32),
-            pltpu.VMEM((NH, 2, 2 * ROWS, HEAD), f32),
-            pltpu.VMEM((NH, 2, 2 * ROWS, HEAD), f32),
+            pltpu.VMEM((NH, NY * ROWS, HEAD), f32),
+            pltpu.VMEM((NH, NY * ROWS, HEAD), f32),
+            pltpu.VMEM((NH, NY * ROWS, HEAD), f32),
             pltpu.VMEM((ROWS, NH * HEAD), bf16),
             pltpu.VMEM((4, ROWS, COLS), f32),
             pltpu.VMEM((4, 8, ROWS), f32),
@@ -466,8 +438,8 @@
             dma((NG,)),
             dma((NG, 2, 4)),
             dma((NG, NZ + 1)),
-            dma((NG, 4)),
-            dma((NG, 4)),
+            dma((NG, 5)),
+            dma((NG, 5)),
             dma((NY,)),
             dma((NY,)),
         ]

time: 70.9 us -> 75.3 us (1.062)
  Pallas kernels: 70.2 us -> 74.6 us
    pallas_call x1, Pallas kernels: 68 us -> 72.4 us  [body(): pl.pallas_call(kernel, out_shape=(jax.ShapeDtypeStruct((ROWS, COLS), f32)...]
where the time goes in v7:
time: 75.3 us; the launch traced here: 75.2 us
  Pallas kernels  74.6 us (99%)
    pallas_call x1, Pallas kernels, body(): pl.pallas_call(kernel, out_shape=(jax.ShapeDtypeStruct((ROWS, COLS), f32)...  72.4 us
    pallas_call x1, Pallas kernels, body(): pl.pallas_call(normalise, out_shape=(out, out), in_specs=[vmem] * 4, out_...  2.16 us

profile of v7, /device:TPU:1, one launch (start us, length us, event | category | flops | bytes accessed | tf_op | source)
XLA Modules:
  0.0 75.2 jit_solution(15212568187142252056)
XLA Ops:
  0.6 72.4 %attention_block.1 = (f32[128,1280]{1,0:T(8,128)}, f32[8,128]{1,0:T(8,128)}) custom-call(bf16[128,640]{1,0:T(8,128)(2,1)} %query_hbm.1, f32[640]{0:T(1024)} %gain_hbm.1, bf16[128,640]{1,0:T(8,128)(2,1)} %keys_hbm.1, bf16[128,640]{1,0:T(8,128)(2,1)} %values_hbm.1, bf16[128,5120]{1,0:T(8,128)(2,1)} %hidden_hbm.1, bf16[640,5120]{1,0:T(8,128)(2,1)} %weight_hbm.1, ...), custom_call_target="tpu_custom_call" | custom-call | tf_op jit(solution)/shard_map/attention_block/pallas_call | solution.py:404
  73.0 2.2 %normalise.1 = (bf16[128,1280]{1,0:T(8,128)(2,1)}, bf16[128,1280]{1,0:T(8,128)(2,1)}) custom-call(f32[128,1280]{1,0:T(8,128)} %get-tuple-element.4.summed, f32[8,128]{1,0:T(8,128)} %get-tuple-element.5.moments, f32[1,5120]{1,0:T(1,128)} %bitcast.6, f32[1,5120]{1,0:T(1,128)} %bitcast.7), custom_call_target="tpu_custom_call" | custom-call | tf_op jit(solution)/shard_map/normalise/pallas_call | solution.py:459

commit v8 on v7

--- a/solution.py
+++ b/solution.py
@@ -13,7 +13,7 @@
 HD = 2560
 ROWS = 128
 NH = 5
-GROUPS = ((0, 1), (1, 1), (2, 2), (4, 1))
+GROUPS = ((0, 1), (1, 2), (3, 1), (4, 1))
 NG = len(GROUPS)
 NZ = 8
 NY = 4
@@ -148,10 +148,9 @@
             src, block(g, s + 1, up), kv_send.at[g, int(up), s], block_sem(g, s + 1, up), z_dev(1 if up else -1)
         )
 
-    shares = ((0, 1), (1, 2), (3, 2), (5, 2), (7, 1))
 
     def pair(g, m):
-        places = pl.ds(*shares[m])
+        places = pl.ds(*PARTS[m])
         return remote(
             kv.at[places, 0, heads(g)], kv.at[places, 1, heads(g)], pair_send.at[g, m], pair_recv.at[g, m], sibling
         )
@@ -164,7 +163,8 @@
                 landed(block(g, s, up), block_sem(g, s, up))
             if s < 4:
                 hop(g, s, up).start()
-        pair(g, s).start()
+        if s > 0:
+            pair(g, s - 1).start()
 
     for g in range(min(2, NG)):
         swap(g)
@@ -178,6 +178,9 @@
     swap(2)
     event(1, 0)
     swap(3)
+    for g in range(2, NG):
+        event(g, 0)
+    event(0, 1)
     for r in range(1, 4):
         sq_copy(4 - r).wait_recv()
     factor = lax.rsqrt((sq[0] + sq[1] + sq[2] + sq[3]) / HD + 1e-06) * SCALE
@@ -192,11 +195,9 @@
 
     for r in range(NY):
         send_query(r)
-    event(2, 0)
-    event(3, 0)
-    event(0, 1)
-    event(1, 1)
-    event(2, 1)
+    for g in range(1, NG):
+        event(g, 1)
+    event(0, 2)
 
     def send_mixed(g, r, wait=False):
         back = (NY - r) % NY
@@ -242,9 +243,7 @@
                 def _(g=g):
                     for due in events.get(g, ()):
                         event(*due)
-                    if part == 0:
-                        pair(g, 0).wait_recv()
-                    pair(g, part + 1).wait_recv()
+                    pair(g, part).wait_recv()
 
             attend(h, part)
             if part == len(PARTS) - 1:
@@ -286,18 +285,15 @@
 
     for r in range(NY):
         landed(qbuf.at[r], q_recv.at[r], r)
-    sweep(0, {2: [(3, 1)], 3: [(0, 2)]})
-    event(1, 2)
-    sweep(1, {2: [(2, 2), (3, 2)], 3: [(0, 3)]})
-    event(1, 3)
-    sweep(2, {2: [(2, 3), (3, 3), (0, 4)], 3: [(1, 4)]})
-    sweep(3, {1: [(2, 4), (3, 4)]})
+    sweep(0, {g: [(g, 2)] for g in range(1, NG)})
+    sweep(1, {g: [(g, 3)] for g in range(NG)})
+    sweep(2, {g: [(g, 4)] for g in range(NG)})
+    sweep(3, {})
     copies[4].wait()
-    combine(0)
-    combine(1)
-    combine(2)
+    for g in range(NG - 1):
+        combine(g)
     project_early()
-    combine(3)
+    combine(NG - 1)
 
     for copy in copies[5:]:
         copy.wait()
@@ -360,7 +356,7 @@
         for up in (True, False):
             for s in range(4):
                 hop(g, s, up).wait_send()
-        for m in range(len(shares)):
+        for m in range(len(PARTS)):
             pair(g, m).wait_send()
         for r in range(NY):
             send_mixed(g, r, wait=True)
@@ -438,8 +434,8 @@
             dma((NG,)),
             dma((NG, 2, 4)),
             dma((NG, NZ + 1)),
-            dma((NG, 5)),
-            dma((NG, 5)),
+            dma((NG, 4)),
+            dma((NG, 4)),
             dma((NY,)),
             dma((NY,)),
         ]

time: 75.3 us -> 73.9 us (0.981)
  Pallas kernels: 74.6 us -> 73.2 us
    pallas_call x1, Pallas kernels: 72.4 us -> 71 us  [body(): pl.pallas_call(kernel, out_shape=(jax.ShapeDtypeStruct((ROWS, COLS), f32)...]
where the time goes in v8:
time: 73.9 us; the launch traced here: 73.8 us
  Pallas kernels  73.2 us (99%)
    pallas_call x1, Pallas kernels, body(): pl.pallas_call(kernel, out_shape=(jax.ShapeDtypeStruct((ROWS, COLS), f32)...  71 us
    pallas_call x1, Pallas kernels, body(): pl.pallas_call(normalise, out_shape=(out, out), in_specs=[vmem] * 4, out_...  2.16 us

profile of v8, /device:TPU:1, one launch (start us, length us, event | category | flops | bytes accessed | tf_op | source)
XLA Modules:
  0.0 73.8 jit_solution(13826170708111242900)
XLA Ops:
  0.6 71.0 %attention_block.1 = (f32[128,1280]{1,0:T(8,128)}, f32[8,128]{1,0:T(8,128)}) custom-call(bf16[128,640]{1,0:T(8,128)(2,1)} %query_hbm.1, f32[640]{0:T(1024)} %gain_hbm.1, bf16[128,640]{1,0:T(8,128)(2,1)} %keys_hbm.1, bf16[128,640]{1,0:T(8,128)(2,1)} %values_hbm.1, bf16[128,5120]{1,0:T(8,128)(2,1)} %hidden_hbm.1, bf16[640,5120]{1,0:T(8,128)(2,1)} %weight_hbm.1, ...), custom_call_target="tpu_custom_call" | custom-call | tf_op jit(solution)/shard_map/attention_block/pallas_call | solution.py:400
  71.7 2.2 %normalise.1 = (bf16[128,1280]{1,0:T(8,128)(2,1)}, bf16[128,1280]{1,0:T(8,128)(2,1)}) custom-call(f32[128,1280]{1,0:T(8,128)} %get-tuple-element.4.summed, f32[8,128]{1,0:T(8,128)} %get-tuple-element.5.moments, f32[1,5120]{1,0:T(1,128)} %bitcast.6, f32[1,5120]{1,0:T(1,128)} %bitcast.7), custom_call_target="tpu_custom_call" | custom-call | tf_op jit(solution)/shard_map/normalise/pallas_call | solution.py:455

commit v9 on v8

--- a/solution.py
+++ b/solution.py
@@ -178,9 +178,6 @@
     swap(2)
     event(1, 0)
     swap(3)
-    for g in range(2, NG):
-        event(g, 0)
-    event(0, 1)
     for r in range(1, 4):
         sq_copy(4 - r).wait_recv()
     factor = lax.rsqrt((sq[0] + sq[1] + sq[2] + sq[3]) / HD + 1e-06) * SCALE
@@ -195,9 +192,12 @@
 
     for r in range(NY):
         send_query(r)
-    for g in range(1, NG):
+    for g in range(2, NG):
+        event(g, 0)
+    for g in range(NG):
         event(g, 1)
-    event(0, 2)
+    for g in range(2):
+        event(g, 2)
 
     def send_mixed(g, r, wait=False):
         back = (NY - r) % NY
@@ -285,9 +285,9 @@
 
     for r in range(NY):
         landed(qbuf.at[r], q_recv.at[r], r)
-    sweep(0, {g: [(g, 2)] for g in range(1, NG)})
-    sweep(1, {g: [(g, 3)] for g in range(NG)})
-    sweep(2, {g: [(g, 4)] for g in range(NG)})
+    sweep(0, {2: [(2, 2)], 3: [(3, 2)]})
+    sweep(1, {0: [(0, 3)], 1: [(1, 3)], 2: [(2, 3)], 3: [(3, 3)]})
+    sweep(2, {0: [(0, 4)], 1: [(1, 4)], 2: [(2, 4)], 3: [(3, 4)]})
     sweep(3, {})
     copies[4].wait()
     for g in range(NG - 1):

time: 73.9 us -> 72.3 us (0.978)
  Pallas kernels: 73.2 us -> 71.6 us
    pallas_call x1, Pallas kernels: 71 us -> 69.4 us  [body(): pl.pallas_call(kernel, out_shape=(jax.ShapeDtypeStruct((ROWS, COLS), f32)...]
where the time goes in v9:
time: 72.3 us; the launch traced here: 72.2 us
  Pallas kernels  71.6 us (99%)
    pallas_call x1, Pallas kernels, body(): pl.pallas_call(kernel, out_shape=(jax.ShapeDtypeStruct((ROWS, COLS), f32)...  69.4 us
    pallas_call x1, Pallas kernels, body(): pl.pallas_call(normalise, out_shape=(out, out), in_specs=[vmem] * 4, out_...  2.16 us

profile of v9, /device:TPU:1, one launch (start us, length us, event | category | flops | bytes accessed | tf_op | source)
XLA Modules:
  0.0 72.2 jit_solution(10210989352489941235)
XLA Ops:
  0.6 69.4 %attention_block.1 = (f32[128,1280]{1,0:T(8,128)}, f32[8,128]{1,0:T(8,128)}) custom-call(bf16[128,640]{1,0:T(8,128)(2,1)} %query_hbm.1, f32[640]{0:T(1024)} %gain_hbm.1, bf16[128,640]{1,0:T(8,128)(2,1)} %keys_hbm.1, bf16[128,640]{1,0:T(8,128)(2,1)} %values_hbm.1, bf16[128,5120]{1,0:T(8,128)(2,1)} %hidden_hbm.1, bf16[640,5120]{1,0:T(8,128)(2,1)} %weight_hbm.1, ...), custom_call_target="tpu_custom_call" | custom-call | tf_op jit(solution)/shard_map/attention_block/pallas_call | solution.py:400
  70.1 2.2 %normalise.1 = (bf16[128,1280]{1,0:T(8,128)(2,1)}, bf16[128,1280]{1,0:T(8,128)(2,1)}) custom-call(f32[128,1280]{1,0:T(8,128)} %get-tuple-element.4.summed, f32[8,128]{1,0:T(8,128)} %get-tuple-element.5.moments, f32[1,5120]{1,0:T(1,128)} %bitcast.6, f32[1,5120]{1,0:T(1,128)} %bitcast.7), custom_call_target="tpu_custom_call" | custom-call | tf_op jit(solution)/shard_map/normalise/pallas_call | solution.py:455
